TPU v7x, 32 devices: a whole 2x2x4 slice. The times are simulated.
32 devices in a mesh: brick: 16 (over z, x, core), pme: 2 (over y).
Axes of the slice: x: 2, y: 2, z: 4, core: 2. Of those that a mesh axis runs over, the one named last changes fastest.
Arguments:
- features: bfloat16 [4096, 512], P(('brick', 'pme')), may hold values from -6 to 6
- cotangent: bfloat16 [4096, 1152], P(('brick', 'pme')), may hold values from -6 to 6
- neighbor_index: int32 [262144], P(('brick', 'pme')), may hold values from 0 to 319
- neighbor_count: int32 [4096], P(('brick', 'pme')), may hold values from 1 to 64, as said below
- edge_vector: float32 [3, 262144], P(None, ('brick', 'pme')), may hold values from -2.7 to 2.7, as said below
- quad_index: int32 [32, 2, 2, 16], P(('brick', 'pme')), may hold values from 0 to 127, as said below
- weight_basis: float32 [8, 64], replicated, may hold values from -2 to 2
- weight_radial: bfloat16 [64, 896], replicated, may hold values from -0.75 to 0.75
- weight_scalar: float32 [128, 128], replicated, may hold values from -0.5 to 0.5
- weight_gate: float32 [128, 256], replicated, may hold values from -0.5 to 0.5
- weight_vector: float32 [128, 128], replicated, may hold values from -0.5 to 0.5
- weight_tensor: float32 [128, 128], replicated, may hold values from -0.5 to 0.5
- weight_charge: float32 [128], replicated, may hold values from -0.5 to 0.5
- grid_base: int32 [3, 4096], P(None, ('brick', 'pme')), may hold values from 0 to 191, as said below
- grid_frac: float32 [3, 4096], P(None, ('brick', 'pme')), may hold values from -0.5 to 0.5
Outputs:
- updated: bfloat16 [4096, 1152], P(('brick', 'pme'))
- feature_grad: float32 [4096, 512], P(('brick', 'pme'))
- potential: float32 [96, 48, 192], P('brick', 'pme')
Inputs may be any that keep to these rules, and one draw needn't show every extreme that they name: `neighbor_index`: values below 128 name the device's own rows; 128 + m * 16 + g names row g of the m-th border block. `neighbor_count`: slots below the count are live, the rest padding; counts cluster by device. `edge_vector`: every component has magnitude between 0.5 and 2.7. `quad_index`: the 64 entries of one device are distinct. `grid_base`: row 0 is below 6, row 1 below 24, row 2 below 192.
All inputs are finite; a program needn't handle non-finite values.
Results may differ from a plain program's by a relative error of at most 0.004.
Values may be sent and summed in bfloat16 or wider, within the bound.
No kernel may reach another device: no remote copies, remote signals or barrier semaphores. Data moves between devices by JAX's collectives and lax.ppermute only.
A program may use at most 128 MiB of HBM per device.

v0:
```python
import functools
import math

import jax
import jax.numpy as jnp
from jax import lax
from jax.experimental import pallas as pl
from jax.experimental.pallas import tpu as pltpu
from jax.sharding import PartitionSpec as P

GX = 6
GY = 24
NGZ = 192

CUTOFF = 5.0
SMEAR = 1.0
COUPLING = 0.1
PRECISE = lax.Precision.HIGHEST
BORDER = ((0, 0), (0, 1), (0, 2), (0, 3), (1, 0), (1, 3), (2, 0), (2, 3), (3, 0), (3, 1), (3, 2), (3, 3))
SHIFT = (-1, 0, 0, 1)
QUARTER = (1, 0, 1, 0)
SLOT_BLOCK = 8
ROW_GROUP = 16
VMEM_LIMIT = 48 * 1024 * 1024


def halo_groups(brick_count, pme_count):
    groups = {}
    for cell, (row, col) in enumerate(BORDER):
        step = (SHIFT[row] % brick_count, SHIFT[col] % pme_count)
        groups.setdefault(step, []).append(cell)
    return tuple((step, tuple(cells)) for step, cells in groups.items())


def shifted(value, brick_step, pme_step):
    bricks, pmes = lax.axis_size("brick"), lax.axis_size("pme")
    pairs = []
    for b in range(bricks):
        for p in range(pmes):
            source = (b + brick_step) % bricks * pmes + (p + pme_step) % pmes
            pairs.append((source, b * pmes + p))
    return lax.ppermute(value, ("brick", "pme"), pairs)


def dot_t(left, right, dims, precision=None):
    return lax.dot_general(
        left, right, (dims, ((), ())), precision=precision, preferred_element_type=jnp.float32
    )


def dot_f32(left, right, dims=((1,), (0,))):
    return dot_t(left, right, dims, PRECISE)


def params(**kwargs):
    return pltpu.CompilerParams(vmem_limit_bytes=VMEM_LIMIT, **kwargs)


def pack_kernel(groups, quad_ref, features_ref, *message_refs):
    atoms = features_ref.shape[0]
    ghost = quad_ref.shape[3]
    rows = lax.broadcasted_iota(jnp.int32, (atoms, ghost), 0)
    picked = {}
    for row in range(2):
        for col in range(2):
            chosen = (rows == quad_ref[0, row, col : col + 1, :]).astype(jnp.bfloat16)
            picked[row, col] = dot_t(chosen, features_ref[...], ((0,), (0,))).astype(jnp.bfloat16)
    for (_, cells), message_ref in zip(groups, message_refs):
        for place, cell in enumerate(cells):
            row, col = BORDER[cell]
            message_ref[place * ghost : (place + 1) * ghost, :] = picked[QUARTER[row], QUARTER[col]]


def radial_kernel(vector_ref, count_ref, basis_weight_ref, hidden_ref, unit_ref, basis_ref):
    slots, atoms = vector_ref.shape[1:]
    orders = basis_weight_ref.shape[0]
    parts = [vector_ref[axis] for axis in range(3)]
    distance = jnp.sqrt(parts[0] * parts[0] + parts[1] * parts[1] + parts[2] * parts[2])
    inverse = 1.0 / distance
    for axis in range(3):
        unit_ref[axis] = parts[axis] * inverse
    theta = distance * (math.pi / CUTOFF)
    cosine = jnp.cos(theta)
    live = lax.broadcasted_iota(jnp.int32, (slots, atoms), 0) < count_ref[...]
    envelope = jnp.where(live, 0.5 * (cosine + 1.0), 0.0)
    before = jnp.zeros_like(theta)
    current = jnp.sin(theta) * envelope
    for order in range(orders):
        for slot in range(slots):
            basis_ref[order : order + 1, slot * atoms : (slot + 1) * atoms] = current[slot : slot + 1, :]
        before, current = current, 2.0 * cosine * current - before
    width = SLOT_BLOCK * atoms
    for start in range(0, slots * atoms, width):
        inner = dot_f32(basis_weight_ref[...], basis_ref[:, start : start + width], ((0,), (0,)))
        hidden_ref[:, start : start + width] = (inner * jax.nn.sigmoid(inner)).astype(jnp.bfloat16)


def load_radial_weight(weight_ref, weight_t_ref):
    channels = weight_ref.shape[1] // 7
    for path in range(7):
        block = weight_ref[:, path * channels : (path + 1) * channels].astype(jnp.float32)
        if path == 3:
            block = block - weight_ref[:, 4 * channels : 5 * channels].astype(jnp.float32) * (1.0 / 3.0)
        weight_t_ref[path * channels : (path + 1) * channels, :] = block.T.astype(jnp.bfloat16)


def sender_onehot(index_ref, table_rows):
    slots, atoms = index_ref.shape
    rows = lax.broadcasted_iota(jnp.int32, (table_rows, atoms), 0)
    return jnp.concatenate(
        [(rows == index_ref[slot : slot + 1, :]).astype(jnp.bfloat16) for slot in range(slots)], axis=1
    )


def forward_kernel(
    groups,
    hidden_ref,
    unit_ref,
    index_ref,
    features_ref,
    weight_radial_ref,
    weight_scalar_ref,
    weight_gate_ref,
    weight_vector_ref,
    weight_tensor_ref,
    weight_charge_ref,
    cotangent_ref,
    *rest,
):
    message_refs = rest[: len(groups)]
    updated_ref, charge_ref, node_grad_ref = rest[len(groups) : len(groups) + 3]
    table_ref, table_t_ref, weight_t_ref, radial_ref, sender_ref, total_ref = rest[len(groups) + 3 :]
    step = pl.program_id(0)
    atoms, width = features_ref.shape
    channels = width // 4
    ghost = (table_ref.shape[0] - atoms) // 12
    slots = index_ref.shape[0]

    @pl.when(step == 0)
    def _():
        table_ref[:atoms, :] = features_ref[...]
        for (_, cells), message_ref in zip(groups, message_refs):
            for place, cell in enumerate(cells):
                lower = atoms + cell * ghost
                table_ref[lower : lower + ghost, :] = message_ref[place * ghost : (place + 1) * ghost, :]
        for block in range(4):
            piece = table_ref[:, block * channels : (block + 1) * channels].astype(jnp.float32)
            table_t_ref[block * channels : (block + 1) * channels, :] = piece.T.astype(jnp.bfloat16)
        load_radial_weight(weight_radial_ref, weight_t_ref)
        total_ref[...] = jnp.zeros_like(total_ref)

    sender_ref[...] = dot_t(
        table_t_ref[...], sender_onehot(index_ref, table_ref.shape[0]), ((1,), (0,))
    )
    radial_ref[...] = dot_t(weight_t_ref[...], hidden_ref[...], ((1,), (0,)))

    def group(number, carry):
        row = pl.multiple_of(number * ROW_GROUP, ROW_GROUP)
        total = [total_ref[block, pl.ds(row, ROW_GROUP), :] for block in range(10)]
        for slot in range(slots):
            lanes = slice(slot * atoms, (slot + 1) * atoms)
            unit = [unit_ref[axis, slot : slot + 1, :] for axis in range(3)]
            paths = [radial_ref[pl.ds(path * channels + row, ROW_GROUP), lanes] for path in range(7)]
            scalar = sender_ref[pl.ds(row, ROW_GROUP), lanes]
            vector = [
                sender_ref[pl.ds((1 + axis) * channels + row, ROW_GROUP), lanes] for axis in range(3)
            ]
            along = unit[0] * vector[0] + unit[1] * vector[1] + unit[2] * vector[2]
            total[0] = total[0] + (paths[0] * scalar + paths[1] * along)
            pushed = paths[2] * scalar + paths[4] * along
            twisted = paths[5] * scalar
            mixed = []
            for axis in range(3):
                total[1 + axis] = total[1 + axis] + (unit[axis] * pushed + paths[3] * vector[axis])
                mixed.append(unit[axis] * twisted + paths[6] * vector[axis])
                total[4 + axis] = total[4 + axis] + unit[axis] * mixed[axis]
            for place, (left, right) in enumerate(((0, 1), (1, 2), (0, 2))):
                total[7 + place] = total[7 + place] + (
                    unit[left] * mixed[right] + unit[right] * mixed[left]
                )
        for block in range(10):
            total_ref[block, pl.ds(row, ROW_GROUP), :] = total[block]
        return carry

    lax.fori_loop(0, channels // ROW_GROUP, group, 0)

    @pl.when(step == pl.num_programs(0) - 1)
    def _():
        scale = 1.0 / math.sqrt(slots * pl.num_programs(0))
        trace = (total_ref[4] + total_ref[5] + total_ref[6]) * (1.0 / 3.0)
        blocks = [total_ref[0], total_ref[1], total_ref[2], total_ref[3]]
        blocks += [total_ref[4] - trace, total_ref[5] - trace]
        blocks += [0.5 * total_ref[7], 0.5 * total_ref[8], 0.5 * total_ref[9]]
        aggregate = [(block * scale).T for block in blocks]
        columns = lambda ref, block: ref[:, block * channels : (block + 1) * channels].astype(jnp.float32)
        gate = jax.nn.sigmoid(dot_f32(aggregate[0], weight_gate_ref[...]))
        inner = dot_f32(aggregate[0], weight_scalar_ref[...])
        inner_sigmoid = jax.nn.sigmoid(inner)
        vectors = dot_f32(jnp.concatenate(aggregate[1:4], axis=0), weight_vector_ref[...])
        tensors = dot_f32(jnp.concatenate(aggregate[4:9], axis=0), weight_tensor_ref[...])
        gate_v, gate_t = gate[:, :channels], gate[:, channels:]
        scalar_out = (columns(features_ref, 0) + inner * inner_sigmoid).astype(jnp.bfloat16)
        updated_ref[:, :channels] = scalar_out
        charge_ref[...] = dot_f32(weight_charge_ref[...], scalar_out.astype(jnp.float32), ((1,), (1,)))
        grad_v, grad_t = [], []
        gate_grad_v = jnp.zeros((atoms, channels), jnp.float32)
        gate_grad_t = jnp.zeros((atoms, channels), jnp.float32)
        for axis in range(3):
            value = vectors[axis * atoms : (axis + 1) * atoms]
            given = columns(cotangent_ref, 1 + axis)
            updated_ref[:, (1 + axis) * channels : (2 + axis) * channels] = (
                columns(features_ref, 1 + axis) + gate_v * value
            ).astype(jnp.bfloat16)
            gate_grad_v = gate_grad_v + given * value
            grad_v.append(given * gate_v)
        for block in range(5):
            value = tensors[block * atoms : (block + 1) * atoms]
            given = columns(cotangent_ref, 4 + block)
            updated_ref[:, (4 + block) * channels : (5 + block) * channels] = (gate_t * value).astype(
                jnp.bfloat16
            )
            gate_grad_t = gate_grad_t + given * value
            grad_t.append(given * gate_t)
        inner_grad = columns(cotangent_ref, 0) * (
            inner_sigmoid * (1.0 + inner * (1.0 - inner_sigmoid))
        )
        gate_grad = jnp.concatenate([gate_grad_v, gate_grad_t], axis=1) * (gate * (1.0 - gate))
        across = ((1,), (1,))
        grad_s = dot_f32(inner_grad, weight_scalar_ref[...], across)
        grad_s = grad_s + dot_f32(gate_grad, weight_gate_ref[...], across)
        grad_v = dot_f32(jnp.concatenate(grad_v, axis=0), weight_vector_ref[...], across)
        grad_t = dot_f32(jnp.concatenate(grad_t, axis=0), weight_tensor_ref[...], across)
        t00, t11, t01, t12, t02 = [grad_t[block * atoms : (block + 1) * atoms] for block in range(5)]
        third = (t00 + t11) * (1.0 / 3.0)
        pieces = [grad_s] + [grad_v[axis * atoms : (axis + 1) * atoms] for axis in range(3)]
        pieces += [t00 - third, t11 - third, -third, 0.5 * t01, 0.5 * t12, 0.5 * t02]
        for block in range(10):
            node_grad_ref[block] = (pieces[block] * scale).T


def backward_kernel(
    groups,
    hidden_ref,
    unit_ref,
    index_ref,
    node_grad_ref,
    weight_radial_ref,
    cotangent_ref,
    own_grad_ref,
    *rest,
):
    message_refs = rest[: len(groups)]
    weight_t_ref, radial_ref, grad_ref, total_ref = rest[len(groups) :]
    step = pl.program_id(0)
    atoms = index_ref.shape[1]
    slots = index_ref.shape[0]
    channels = node_grad_ref.shape[1]
    table_rows = total_ref.shape[0]
    ghost = (table_rows - atoms) // 12

    @pl.when(step == 0)
    def _():
        load_radial_weight(weight_radial_ref, weight_t_ref)
        total_ref[...] = jnp.zeros_like(total_ref)

    radial_ref[...] = dot_t(weight_t_ref[...], hidden_ref[...], ((1,), (0,)))

    def group(number, carry):
        row = pl.multiple_of(number * ROW_GROUP, ROW_GROUP)
        node = [node_grad_ref[block, pl.ds(row, ROW_GROUP), :] for block in range(10)]
        g_s, g_v, diag, off = node[0], node[1:4], node[4:7], {(0, 1): node[7], (1, 2): node[8], (0, 2): node[9]}
        for slot in range(slots):
            lanes = slice(slot * atoms, (slot + 1) * atoms)
            unit = [unit_ref[axis, slot : slot + 1, :] for axis in range(3)]
            paths = [radial_ref[pl.ds(path * channels + row, ROW_GROUP), lanes] for path in range(7)]
            along = unit[0] * g_v[0] + unit[1] * g_v[1] + unit[2] * g_v[2]
            bent = [
                unit[0] * diag[0] + unit[1] * off[0, 1] + unit[2] * off[0, 2],
                unit[0] * off[0, 1] + unit[1] * diag[1] + unit[2] * off[1, 2],
                unit[0] * off[0, 2] + unit[1] * off[1, 2] + unit[2] * diag[2],
            ]
            twice = unit[0] * bent[0] + unit[1] * bent[1] + unit[2] * bent[2]
            scalar = paths[0] * g_s + paths[2] * along + paths[5] * twice
            pushed = paths[1] * g_s + paths[4] * along
            grad_ref[pl.ds(row, ROW_GROUP), lanes] = scalar.astype(jnp.bfloat16)
            for axis in range(3):
                vector = unit[axis] * pushed + paths[3] * g_v[axis] + paths[6] * bent[axis]
                grad_ref[pl.ds((1 + axis) * channels + row, ROW_GROUP), lanes] = vector.astype(jnp.bfloat16)
        return carry

    lax.fori_loop(0, channels // ROW_GROUP, group, 0)
    total_ref[...] += dot_t(sender_onehot(index_ref, table_rows), grad_ref[...], ((1,), (1,)))

    @pl.when(step == pl.num_programs(0) - 1)
    def _():
        own_grad_ref[...] = total_ref[:atoms, :] + cotangent_ref[:, : 4 * channels].astype(jnp.float32)
        for (_, cells), message_ref in zip(groups, message_refs):
            for place, cell in enumerate(cells):
                lower = atoms + cell * ghost
                message_ref[place * ghost : (place + 1) * ghost, :] = total_ref[
                    lower : lower + ghost, :
                ].astype(jnp.bfloat16)


def gather_kernel(groups, quad_ref, own_ref, *rest):
    message_refs, out_ref = rest[: len(groups)], rest[len(groups)]
    atoms = own_ref.shape[0]
    ghost = quad_ref.shape[3]
    rows = lax.broadcasted_iota(jnp.int32, (atoms, ghost), 0)
    total = own_ref[...]
    for (_, cells), message_ref in zip(groups, message_refs):
        for place, cell in enumerate(cells):
            row, col = QUARTER[BORDER[cell][0]], QUARTER[BORDER[cell][1]]
            chosen = (rows == quad_ref[0, row, col : col + 1, :]).astype(jnp.bfloat16)
            total = total + dot_t(chosen, message_ref[place * ghost : (place + 1) * ghost, :], ((1,), (0,)))
    out_ref[...] = total


def whole(shape):
    return pl.BlockSpec(shape, lambda step: (0,) * len(shape))


def for_sending(array):
    return jax.tree.map(lambda a: a.astype(jnp.bfloat16) if a.dtype == jnp.float32 else a, array)


def passed_along(value, axis, steps):
    count = lax.axis_size(axis)
    pairs = [(source, (source + steps) % count) for source in range(count)]
    return lax.ppermute(value, axis, pairs)


def spline_weights(offset):
    return (
        0.5 * (0.5 - offset) * (0.5 - offset),
        0.75 - offset * offset,
        0.5 * (0.5 + offset) * (0.5 + offset),
    )


def spline_table(base_cell, offset, points, wrapped):
    positions = jnp.arange(points, dtype=jnp.int32)[None, :]
    summed = jnp.zeros((base_cell.shape[0], points), jnp.float32)
    for step_id, weight in zip((-1, 0, 1), spline_weights(offset)):
        if wrapped:
            target = (base_cell + step_id) % points
        else:
            target = base_cell + step_id + 1
        summed = summed + weight[:, None] * (positions == target[:, None]).astype(jnp.float32)
    return summed


def influence(index_x, index_y, index_z, points_x, points_y, points_z):
    summed = 0.0
    correct = 1.0
    for index_k, points in ((index_x, points_x), (index_y, points_y), (index_z, points_z)):
        folded = jnp.minimum(index_k, points - index_k).astype(jnp.float32) / points
        modulus = 0.75 + 0.25 * jnp.cos(2.0 * jnp.pi / points * index_k.astype(jnp.float32))
        summed = summed + folded * folded
        correct = correct / (modulus * modulus)
    nonzero = summed > 0.0
    safe_sum = jnp.where(nonzero, summed, 1.0)
    value = COUPLING * jnp.exp(-2.0 * jnp.pi * jnp.pi * SMEAR * SMEAR * summed) / safe_sum * correct
    return jnp.where(nonzero, value, 0.0)


def hartley(points):
    positions = jnp.arange(points, dtype=jnp.int32)
    phase = positions[:, None] * positions[None, :] % points
    angle = phase.astype(jnp.float32) * (2.0 * jnp.pi / points)
    return jnp.cos(angle) + jnp.sin(angle)


def solve_potential(charge_grid, cells_x, cells_y, cells_z):
    full_x = cells_x * lax.axis_size("brick")
    full_y = cells_y * lax.axis_size("pme")
    part_y = full_y // lax.axis_size("brick")
    part_z = cells_z // lax.axis_size("pme")
    table_x = hartley(full_x)
    table_y = hartley(full_y)
    table_z = hartley(cells_z)
    spectrum = jnp.dot(charge_grid.reshape(-1, cells_z), table_z, precision=PRECISE).reshape(
        cells_x, cells_y, cells_z
    )
    spectrum = lax.all_to_all(
        for_sending(spectrum), "pme", split_axis=2, concat_axis=1, tiled=True
    ).astype(spectrum.dtype)
    spectrum = jnp.einsum("xyz,yk->xkz", spectrum, table_y, precision=PRECISE)
    spectrum = lax.all_to_all(spectrum, "brick", split_axis=1, concat_axis=0, tiled=True)
    spectrum = jnp.dot(table_x, spectrum.reshape(full_x, -1), precision=PRECISE).reshape(
        full_x, part_y, part_z
    )
    index_x = jnp.arange(full_x, dtype=jnp.int32)[:, None, None]
    index_y = lax.axis_index("brick") * part_y + jnp.arange(part_y, dtype=jnp.int32)[None, :, None]
    index_z = lax.axis_index("pme") * part_z + jnp.arange(part_z, dtype=jnp.int32)[None, None, :]
    spectrum = spectrum * influence(index_x, index_y, index_z, full_x, full_y, cells_z)
    spectrum = jnp.dot(table_x, spectrum.reshape(full_x, -1), precision=PRECISE).reshape(
        full_x, part_y, part_z
    )
    spectrum = lax.all_to_all(spectrum, "brick", split_axis=0, concat_axis=1, tiled=True)
    spectrum = jnp.einsum("xyz,yk->xkz", spectrum, table_y, precision=PRECISE)
    spectrum = lax.all_to_all(spectrum, "pme", split_axis=1, concat_axis=2, tiled=True)
    spectrum = jnp.dot(spectrum.reshape(-1, cells_z), table_z, precision=PRECISE).reshape(
        cells_x, cells_y, cells_z
    )
    return spectrum * (1.0 / (full_x * full_y * cells_z))


def fold_grid(charge_patch, cells_x, cells_y):
    for shift_by in (1, -1):
        source_plane = cells_x + 1 if shift_by == 1 else 0
        target_plane = 1 if shift_by == 1 else cells_x
        arrived = passed_along(charge_patch[source_plane], "brick", shift_by)
        charge_patch = charge_patch.at[target_plane].add(arrived)
    for shift_by in (1, -1):
        source_line = cells_y + 1 if shift_by == 1 else 0
        target_line = 1 if shift_by == 1 else cells_y
        arrived = passed_along(charge_patch[1 : cells_x + 1, source_line], "pme", shift_by)
        charge_patch = charge_patch.at[1 : cells_x + 1, target_line].add(arrived)
    return charge_patch[1 : cells_x + 1, 1 : cells_y + 1]


def per_device(
    features,
    cotangent,
    neighbor_index,
    neighbor_count,
    edge_vector,
    quad_index,
    weight_basis,
    weight_radial,
    weight_scalar,
    weight_gate,
    weight_vector,
    weight_tensor,
    weight_charge,
    grid_base,
    grid_frac,
):
    atoms, width = features.shape
    channels = width // 4
    slots = neighbor_index.shape[0] // atoms
    ghost = quad_index.shape[3]
    table_rows = atoms + 12 * ghost
    hidden_units = weight_basis.shape[1]
    groups = halo_groups(lax.axis_size("brick"), lax.axis_size("pme"))
    message_shapes = [
        jax.ShapeDtypeStruct((len(cells) * ghost, width), jnp.bfloat16) for _, cells in groups
    ]

    outgoing = pl.pallas_call(
        functools.partial(pack_kernel, groups), out_shape=message_shapes, name="pack"
    )(quad_index, features)
    incoming = [shifted(value, *steps) for (steps, _), value in zip(groups, outgoing)]

    index_t = neighbor_index.reshape(atoms, slots).T
    vector_t = edge_vector.reshape(3, atoms, slots).transpose(0, 2, 1)
    hidden, unit = pl.pallas_call(
        radial_kernel,
        out_shape=[
            jax.ShapeDtypeStruct((hidden_units, slots * atoms), jnp.bfloat16),
            jax.ShapeDtypeStruct((3, slots, atoms), jnp.float32),
        ],
        scratch_shapes=[pltpu.VMEM((weight_basis.shape[0], slots * atoms), jnp.float32)],
        compiler_params=params(),
        name="radial",
    )(vector_t, neighbor_count.reshape(1, atoms), weight_basis)

    block = SLOT_BLOCK * atoms
    edge_specs = [
        pl.BlockSpec((hidden_units, block), lambda step: (0, step)),
        pl.BlockSpec((3, SLOT_BLOCK, atoms), lambda step: (0, step, 0)),
        pl.BlockSpec((SLOT_BLOCK, atoms), lambda step: (step, 0)),
    ]
    weights = (weight_radial, weight_scalar, weight_gate, weight_vector, weight_tensor)
    charge_weight = weight_charge.reshape(1, channels)
    forward_shapes = [
        jax.ShapeDtypeStruct((atoms, 9 * channels), jnp.bfloat16),
        jax.ShapeDtypeStruct((1, atoms), jnp.float32),
        jax.ShapeDtypeStruct((10, channels, atoms), jnp.float32),
    ]
    updated, charge, node_grad = pl.pallas_call(
        functools.partial(forward_kernel, groups),
        grid=(slots // SLOT_BLOCK,),
        in_specs=edge_specs
        + [whole(features.shape)]
        + [whole(w.shape) for w in weights]
        + [whole(charge_weight.shape), whole(cotangent.shape)]
        + [whole(shape.shape) for shape in message_shapes],
        out_specs=[whole(shape.shape) for shape in forward_shapes],
        out_shape=forward_shapes,
        scratch_shapes=[
            pltpu.VMEM((table_rows, width), jnp.bfloat16),
            pltpu.VMEM((width, table_rows), jnp.bfloat16),
            pltpu.VMEM((7 * channels, hidden_units), jnp.bfloat16),
            pltpu.VMEM((7 * channels, block), jnp.float32),
            pltpu.VMEM((width, block), jnp.float32),
            pltpu.VMEM((10, channels, atoms), jnp.float32),
        ],
        compiler_params=params(),
        name="forward",
    )(hidden, unit, index_t, features, *weights, charge_weight, cotangent, *incoming)
    charge = charge.reshape(atoms)

    own_grad, *ghost_grads = pl.pallas_call(
        functools.partial(backward_kernel, groups),
        grid=(slots // SLOT_BLOCK,),
        in_specs=edge_specs
        + [whole((10, channels, atoms)), whole(weight_radial.shape), whole(cotangent.shape)],
        out_specs=[whole((atoms, width))] + [whole(shape.shape) for shape in message_shapes],
        out_shape=[jax.ShapeDtypeStruct((atoms, width), jnp.float32)] + message_shapes,
        scratch_shapes=[
            pltpu.VMEM((7 * channels, hidden_units), jnp.bfloat16),
            pltpu.VMEM((7 * channels, block), jnp.float32),
            pltpu.VMEM((width, block), jnp.bfloat16),
            pltpu.VMEM((table_rows, width), jnp.float32),
        ],
        compiler_params=params(),
        name="backward",
    )(hidden, unit, index_t, node_grad, weight_radial, cotangent)
    returned = [shifted(value, -steps[0], -steps[1]) for (steps, _), value in zip(groups, ghost_grads)]
    feature_grad = pl.pallas_call(
        functools.partial(gather_kernel, groups),
        out_shape=jax.ShapeDtypeStruct((atoms, width), jnp.float32),
        name="gather",
    )(quad_index, own_grad, *returned)

    cells_x = GX
    cells_y = GY
    cells_z = NGZ
    table_x = spline_table(grid_base[0], grid_frac[0], cells_x + 2, False)
    table_y = spline_table(grid_base[1], grid_frac[1], cells_y + 2, False)
    table_z = spline_table(grid_base[2], grid_frac[2], cells_z, True)
    plane_rows = (table_x[:, :, None] * table_y[:, None, :] * charge[:, None, None]).reshape(
        atoms, -1
    )
    spread_grid = lax.dot_general(plane_rows, table_z, (((0,), (0,)), ((), ())), precision=PRECISE)
    charge_patch = spread_grid.reshape(cells_x + 2, cells_y + 2, cells_z)
    charge_grid = fold_grid(charge_patch, cells_x, cells_y)
    potential = solve_potential(charge_grid, cells_x, cells_y, cells_z)
    return (updated, feature_grad, potential)


def solution(mesh):
    placed = (
        P(("brick", "pme"), None),
        P(("brick", "pme"), None),
        P(("brick", "pme")),
        P(("brick", "pme")),
        P(None, ("brick", "pme")),
        P(("brick", "pme"), None, None, None),
        P(),
        P(),
        P(),
        P(),
        P(),
        P(),
        P(),
        P(None, ("brick", "pme")),
        P(None, ("brick", "pme")),
    )
    return jax.shard_map(
        per_device,
        mesh=mesh,
        in_specs=placed,
        out_specs=(P(("brick", "pme"), None), P(("brick", "pme"), None), P("brick", "pme", None)),
        check_vma=False,
    )
```

profile of v0, /device:TPU:0, one launch (start us, length us, event | category | flops | bytes accessed | tf_op | source)
XLA Modules:
  0.0 125.5 jit_solution(15814087548012669297)
XLA Ops:
  0.7 1.8 %pack.1 = (bf16[32,512]{1,0:T(8,128)(2,1)}, bf16[32,512]{1,0:T(8,128)(2,1)}, bf16[64,512]{1,0:T(8,128)(2,1)}, bf16[32,512]{1,0:T(8,128)(2,1)}, bf16[32,512]{1,0:T(8,128)(2,1)}) custom-call(s32[1,2,2,16]{3,2,1,0:T(2,128)} %quad_ref.3, bf16[128,512]{1,0:T(8,128)(2,1)} %features_ref.3), custom_call_target="tpu_custom_call" | custom-call | tf_op jit(solution)/shard_map/pack/pallas_call | solution.py:451
  2.5 2.4 %collective-permute-start = (bf16[32,512]{1,0:T(8,128)(2,1)}, bf16[32,512]{1,0:T(8,128)(2,1)S(1)}, u32[]{:S(2)}, u32[]{:S(2)}) collective-permute-start(bf16[32,512]{1,0:T(8,128)(2,1)} %get-tuple-element.69), channel_id=1, source_target_pairs={{31,0},{30,1},{1,2},{0,3},{3,4},{2,5},{5,6},{4,7},{7,8},{6,9},{9,1... | collective-permute-start | bytes 98312 | tf_op jit(solution)/shard_map/ppermute | solution.py:42
  4.9 1.6 %collective-permute-start.1 = (bf16[32,512]{1,0:T(8,128)(2,1)}, bf16[32,512]{1,0:T(8,128)(2,1)S(1)}, u32[]{:S(2)}, u32[]{:S(2)}) collective-permute-start(bf16[32,512]{1,0:T(8,128)(2,1)} %get-tuple-element.70), channel_id=1, source_target_pairs={{30,0},{31,1},{0,2},{1,3},{2,4},{3,5},{4,6},{5,7},{6,8},{7,9},{8,1... | collective-permute-start | bytes 98312 | tf_op jit(solution)/shard_map/ppermute | solution.py:42
  6.5 0.5 collective-permute-start.2
  7.0 3.5 %collective-permute-start.3 = (bf16[32,512]{1,0:T(8,128)(2,1)}, bf16[32,512]{1,0:T(8,128)(2,1)S(1)}, u32[]{:S(2)}, u32[]{:S(2)}) collective-permute-start(bf16[32,512]{1,0:T(8,128)(2,1)} %get-tuple-element.72), channel_id=1, source_target_pairs={{3,0},{2,1},{5,2},{4,3},{7,4},{6,5},{9,6},{8,7},{11,8},{10,9},{13,... | collective-permute-start | bytes 98312 | tf_op jit(solution)/shard_map/ppermute | solution.py:42
  10.5 1.0 collective-permute-start.4
  11.6 0.2 reshape.679
  11.8 0.1 copy.41
  11.9 0.6 copy-done.13
  12.5 0.1 reshape.681
  12.7 0.6 copy-done.8
  13.4 1.9 %radial.1 = (bf16[64,8192]{1,0:T(8,128)(2,1)S(1)}, f32[3,64,128]{2,1,0:T(8,128)S(1)}) custom-call(f32[3,64,128]{2,1,0:T(8,128)S(1)} %bitcast.104, s32[1,128]{1,0:T(1,128)S(1)} %bitcast.107, f32[8,64]{1,0:T(8,128)S(1)} %copy-done.8), custom_call_target="tpu_custom_call" | custom-call | tf_op jit(solution)/shard_map/radial/pallas_call | solution.py:458
  15.4 0.6 copy-done.10
  16.0 21.0 %forward.1 = (bf16[128,1152]{1,0:T(8,128)(2,1)}, f32[1,128]{1,0:T(1,128)S(1)}, f32[10,128,128]{2,1,0:T(8,128)S(1)}) custom-call(bf16[64,8192]{1,0:T(8,128)(2,1)S(1)} %get-tuple-element.67.hidden_ref, f32[3,64,128]{2,1,0:T(8,128)S(1)} %get-tuple-element.68.unit_ref, s32[64,128]{1,0:T(8,128)S(1)} %bitcast.105, bf16[128,512]{1,0:T(8,128)(2,1)S(1)} %copy-done.1, ...), custom_call_target="tpu_custom_call" | custom-call | tf_op jit(solution)/shard_map/forward/pallas_call | solution.py:482
  36.9 0.6 fusion.14
  37.5 0.1 slice.149
  37.7 0.1 copy.43
  37.9 6.5 %collective-permute-done.10 = f32[26,192]{0,1:T(8,128)S(1)} collective-permute-done((f32[26,192]{0,1:T(8,128)S(1)}, f32[26,192]{0,1:T(8,128)S(1)}, u32[]{:S(2)}, u32[]{:S(2)}) %collective-permute-start.10) | collective-permute-done | bytes 20000 | tf_op jit(solution)/shard_map/ppermute | solution.py:330
  44.4 0.1 fusion.21
  44.5 0.1 copy.44
  44.7 0.1 copy.46
  44.8 1.4 %collective-permute-done.11 = f32[26,192]{1,0:T(8,128)S(1)} collective-permute-done((f32[26,192]{1,0:T(8,128)S(1)}, f32[26,192]{1,0:T(8,128)S(1)}, u32[]{:S(2)}, u32[]{:S(2)}) %collective-permute-start.11) | collective-permute-done | bytes 20000 | tf_op jit(solution)/shard_map/ppermute | solution.py:330
  46.3 0.1 scatter-add.15
  46.4 0.6 collective-permute-start.12
  47.0 0.1 broadcast_divide_fusion
  47.1 3.1 %collective-permute-done.12 = f32[6,192]{1,0:T(8,128)S(1)} collective-permute-done((f32[6,192]{1,0:T(8,128)S(1)}, f32[6,192]{1,0:T(8,128)S(1)}, u32[]{:S(2)}, u32[]{:S(2)}) %collective-permute-start.12) | collective-permute-done | bytes 4640 | tf_op jit(solution)/shard_map/ppermute | solution.py:330
  50.2 0.1 scatter-add.16
  50.3 0.6 collective-permute-start.13
  51.0 3.0 %collective-permute-done.13 = f32[6,192]{1,0:T(8,128)S(1)} collective-permute-done((f32[6,192]{1,0:T(8,128)S(1)}, f32[6,192]{1,0:T(8,128)S(1)}, u32[]{:S(2)}, u32[]{:S(2)}) %collective-permute-start.13) | collective-permute-done | bytes 4640 | tf_op jit(solution)/shard_map/ppermute | solution.py:330
  54.1 1.1 convolution_convert_fusion
  55.2 0.2 copy.49
  55.5 1.0 reshape.694
  56.5 3.3 %all-to-all-start = ((bf16[2,2,6912]{2,1,0:T(2,128)(2,1)}), bf16[2,2,6912]{2,1,0:T(2,128)(2,1)S(1)}, u32[]{:S(2)}, u32[]{:S(2)}) async-start(bf16[2,2,6912]{2,1,0:T(2,128)(2,1)} %reshape.694), calls=%async_computation | async-start | bytes 110592 | tf_op jit(solution)/shard_map/all_to_all | solution.py:385
  59.8 4.0 %all-to-all-done = bf16[2,2,6912]{2,1,0:T(2,128)(2,1)S(1)} async-done(((bf16[2,2,6912]{2,1,0:T(2,128)(2,1)}), bf16[2,2,6912]{2,1,0:T(2,128)(2,1)S(1)}, u32[]{:S(2)}, u32[]{:S(2)}) %all-to-all-start) | async-done | bytes 55328 | tf_op jit(solution)/shard_map/all_to_all | solution.py:385
  63.8 0.4 reshape.695
  64.2 0.2 copy.50
  64.5 0.3 convolution_bitcast_fusion.1
  64.8 0.7 copy.51
  65.5 3.5 %all-to-all-start.1 = ((f32[6,48,96]{2,0,1:T(8,128)}), f32[6,48,96]{2,0,1:T(8,128)S(1)}, u32[]{:S(2)}, u32[]{:S(2)}) async-start(f32[6,48,96]{2,0,1:T(8,128)} %copy.51), calls=%async_computation.1 | async-start | bytes 393216 | tf_op jit(solution)/shard_map/all_to_all | solution.py:389
  69.0 0.1 broadcast_add_fusion
  69.1 8.9 %all-to-all-done.1 = f32[6,48,96]{2,0,1:T(8,128)S(1)} async-done(((f32[6,48,96]{2,0,1:T(8,128)}), f32[6,48,96]{2,0,1:T(8,128)S(1)}, u32[]{:S(2)}, u32[]{:S(2)}) %all-to-all-start.1) | async-done | bytes 110624 | tf_op jit(solution)/shard_map/all_to_all | solution.py:389
  78.1 0.1 reshape.687
  78.2 0.1 copy.54
  78.3 0.6 convolution_multiply_fusion
  78.9 0.1 copy.55
  79.0 0.6 fusion.12
  79.6 0.8 copy.56
  80.4 3.7 %all-to-all-start.2 = ((f32[96,3,96]{2,1,0:T(4,128)}), f32[96,3,96]{2,1,0:T(4,128)S(1)}, u32[]{:S(2)}, u32[]{:S(2)}) async-start(f32[96,3,96]{2,1,0:T(4,128)} %copy.56), calls=%async_computation.2 | async-start | bytes 393216 | tf_op jit(solution)/shard_map/all_to_all | solution.py:400
  84.1 17.7 %backward.1 = (f32[128,512]{1,0:T(8,128)S(1)}, bf16[32,512]{1,0:T(8,128)(2,1)S(1)}, bf16[32,512]{1,0:T(8,128)(2,1)S(1)}, bf16[64,512]{1,0:T(8,128)(2,1)S(1)}, bf...) custom-call(bf16[64,8192]{1,0:T(8,128)(2,1)S(1)} %get-tuple-element.67.hidden_ref, ...), custom_call_target="tpu_custom_call" | custom-call | tf_op jit(solution)/shard_map/backward/pallas_call | solution.py:505
  101.8 0.7 copy-done.3
  102.6 0.1 copy.58
  102.8 0.4 convolution_bitcast_fusion
  103.2 0.7 copy.59
  103.9 3.4 %all-to-all-start.3 = ((f32[6,48,96]{2,0,1:T(8,128)}), f32[6,48,96]{2,0,1:T(8,128)S(1)}, u32[]{:S(2)}, u32[]{:S(2)}) async-start(f32[6,48,96]{2,0,1:T(8,128)} %copy.59), calls=%async_computation.3 | async-start | bytes 393216 | tf_op jit(solution)/shard_map/all_to_all | solution.py:402
  107.3 5.5 %collective-permute-start.5 = (bf16[32,512]{1,0:T(8,128)(2,1)S(1)}, bf16[32,512]{1,0:T(8,128)(2,1)S(1)}, u32[]{:S(2)}, u32[]{:S(2)}) collective-permute-start(bf16[32,512]{1,0:T(8,128)(2,1)S(1)} %get-tuple-element.77), channel_id=1, source_target_pairs={{3,0},{2,1},{5,2},{4,3},{7,4},{6,5},{9,6},{8,7},{11,8},{10,9},{13,... | collective-permute-start | bytes 98312 | tf_op jit(solution)/shard_map/ppermute | solution.py:42
  112.9 0.8 collective-permute-start.6
  113.7 0.8 collective-permute-done.5.rest_0_
  114.5 0.8 collective-permute-done.6.rest_1_
  115.3 5.3 %collective-permute-done.8.rest_3_ = bf16[32,512]{1,0:T(8,128)(2,1)S(1)} collective-permute-done((bf16[32,512]{1,0:T(8,128)(2,1)S(1)}, bf16[32,512]{1,0:T(8,128)(2,1)S(1)}, u32[]{:S(2)}, u32[]{:S(2)}) %collective-permute-start.8) | collective-permute-done | bytes 32800 | tf_op jit(solution)/shard_map/ppermute | solution.py:42
  120.7 0.6 copy-done.16
  121.3 2.2 %gather.1 = f32[128,512]{1,0:T(8,128)} custom-call(s32[1,2,2,16]{3,2,1,0:T(2,128)} %quad_ref.3, f32[128,512]{1,0:T(8,128)} %copy-done.3, bf16[32,512]{1,0:T(8,128)(2,1)} %copy-done.14, bf16[32,512]{1,0:T(8,128)(2,1)} %copy-done.15, bf16[64,512]{1,0:T(8,128)(2,1)} %copy-done.12, bf16[32,512]{1,0:T(8,128)(2,1)} %copy-done.16, bf16[32,512]{1,0:T(8,128)(2,1)} %copy-done.17), custom_call_target="tpu_custom_call" | custom-call | tf_op jit(solution)/shard_map/gather/pallas_call | solution.py:522
  123.5 0.1 copy.71
  123.6 0.1 dot_general.41
  123.8 1.8 %convolution_multiply_fusion.1 = f32[6,24,192]{2,1,0:T(8,128)} fusion(f32[6,24,192]{2,1,0:T(8,128)S(1)} %dot_general.41), kind=kOutput, calls=%fused_computation.2 | convolution fusion | flops 64097280 | bytes 221184 | tf_op jit(solution)/shard_map/dot_general | solution.py:403
  (75 shorter events, 1.0 us)
Async XLA Ops:
  0.6 10.8 %copy-start.18 = (f32[3,128]{1,0:T(4,128)S(1)}, f32[3,128]{1,0:T(4,128)}, u32[]{:S(2)}) copy-start(f32[3,128]{1,0:T(4,128)} %param.37) | copy-start | bytes 4612
  0.6 10.8 %copy-start.19 = (s32[3,128]{1,0:T(4,128)S(1)}, s32[3,128]{1,0:T(4,128)}, u32[]{:S(2)}) copy-start(s32[3,128]{1,0:T(4,128)} %param.36) | copy-start | bytes 4612
  2.5 9.1 %copy-start.11 = (f32[3,8192]{1,0:T(4,128)S(1)}, f32[3,8192]{1,0:T(4,128)}, u32[]{:S(2)}) copy-start(f32[3,8192]{1,0:T(4,128)} %param.27) | copy-start | bytes 294916
  2.5 12.8 %collective-permute-start = (bf16[32,512]{1,0:T(8,128)(2,1)}, bf16[32,512]{1,0:T(8,128)(2,1)S(1)}, u32[]{:S(2)}, u32[]{:S(2)}) collective-permute-start(bf16[32,512]{1,0:T(8,128)(2,1)} %get-tuple-element.69), channel_id=1, source_target_pairs={{31,0},{30,1},{1,2},{0,3},{3,4},{2,5},{5,6},{4,7},{7,8},{6,9},{9,1... | collective-permute-start | bytes 98312 | tf_op jit(solution)/shard_map/ppermute | solution.py:42
  4.9 10.4 %collective-permute-start.1 = (bf16[32,512]{1,0:T(8,128)(2,1)}, bf16[32,512]{1,0:T(8,128)(2,1)S(1)}, u32[]{:S(2)}, u32[]{:S(2)}) collective-permute-start(bf16[32,512]{1,0:T(8,128)(2,1)} %get-tuple-element.70), channel_id=1, source_target_pairs={{30,0},{31,1},{0,2},{1,3},{2,4},{3,5},{4,6},{5,7},{6,8},{7,9},{8,1... | collective-permute-start | bytes 98312 | tf_op jit(solution)/shard_map/ppermute | solution.py:42
  6.5 8.8 %collective-permute-start.2 = (bf16[64,512]{1,0:T(8,128)(2,1)}, bf16[64,512]{1,0:T(8,128)(2,1)S(1)}, u32[]{:S(2)}, u32[]{:S(2)}) collective-permute-start(bf16[64,512]{1,0:T(8,128)(2,1)} %get-tuple-element.71), channel_id=1, source_target_pairs={{1,0},{0,1},{3,2},{2,3},{5,4},{4,5},{7,6},{6,7},{9,8},{8,9},{11,10... | collective-permute-start | bytes 196616 | tf_op jit(solution)/shard_map/ppermute | solution.py:42
  7.0 8.3 %collective-permute-start.3 = (bf16[32,512]{1,0:T(8,128)(2,1)}, bf16[32,512]{1,0:T(8,128)(2,1)S(1)}, u32[]{:S(2)}, u32[]{:S(2)}) collective-permute-start(bf16[32,512]{1,0:T(8,128)(2,1)} %get-tuple-element.72), channel_id=1, source_target_pairs={{3,0},{2,1},{5,2},{4,3},{7,4},{6,5},{9,6},{8,7},{11,8},{10,9},{13,... | collective-permute-start | bytes 98312 | tf_op jit(solution)/shard_map/ppermute | solution.py:42
  10.5 4.8 %collective-permute-start.4 = (bf16[32,512]{1,0:T(8,128)(2,1)}, bf16[32,512]{1,0:T(8,128)(2,1)S(1)}, u32[]{:S(2)}, u32[]{:S(2)}) collective-permute-start(bf16[32,512]{1,0:T(8,128)(2,1)} %get-tuple-element.73), channel_id=1, source_target_pairs={{2,0},{3,1},{4,2},{5,3},{6,4},{7,5},{8,6},{9,7},{10,8},{11,9},{12,... | collective-permute-start | bytes 98312 | tf_op jit(solution)/shard_map/ppermute | solution.py:42
  11.6 3.7 %copy-start.7 = (f32[128,128]{1,0:T(8,128)S(1)}, f32[128,128]{1,0:T(8,128)}, u32[]{:S(2)}) copy-start(f32[128,128]{1,0:T(8,128)} %weight_tensor_ref.1) | copy-start | bytes 196612
  11.8 0.8 copy-start.13
  11.8 3.6 %copy-start.4 = (f32[128,256]{1,0:T(8,128)S(1)}, f32[128,256]{1,0:T(8,128)}, u32[]{:S(2)}) copy-start(f32[128,256]{1,0:T(8,128)} %weight_gate_ref.1) | copy-start | bytes 393220
  11.8 3.6 %copy-start.5 = (f32[128,128]{1,0:T(8,128)S(1)}, f32[128,128]{1,0:T(8,128)}, u32[]{:S(2)}) copy-start(f32[128,128]{1,0:T(8,128)} %weight_scalar_ref.1) | copy-start | bytes 196612
  11.8 3.6 %copy-start.6 = (f32[128,128]{1,0:T(8,128)S(1)}, f32[128,128]{1,0:T(8,128)}, u32[]{:S(2)}) copy-start(f32[128,128]{1,0:T(8,128)} %weight_vector_ref.1) | copy-start | bytes 196612
  12.5 2.8 %copy-start = (bf16[128,1152]{1,0:T(8,128)(2,1)S(1)}, bf16[128,1152]{1,0:T(8,128)(2,1)}, u32[]{:S(2)}) copy-start(bf16[128,1152]{1,0:T(8,128)(2,1)} %cotangent_ref.3) | copy-start | bytes 884740
  12.7 0.7 copy-start.8
  12.7 0.7 copy-start.9
  12.7 2.7 %copy-start.1 = (bf16[128,512]{1,0:T(8,128)(2,1)S(1)}, bf16[128,512]{1,0:T(8,128)(2,1)}, u32[]{:S(2)}) copy-start(bf16[128,512]{1,0:T(8,128)(2,1)} %features_ref.3) | copy-start | bytes 393220
  12.7 2.6 %copy-start.2 = (bf16[64,896]{1,0:T(8,128)(2,1)S(1)}, bf16[64,896]{1,0:T(8,128)(2,1)}, u32[]{:S(2)}) copy-start(bf16[64,896]{1,0:T(8,128)(2,1)} %weight_radial_ref.3) | copy-start | bytes 344068
  15.3 0.7 copy-start.10
  37.6 6.8 %collective-permute-start.10 = (f32[26,192]{0,1:T(8,128)S(1)}, f32[26,192]{0,1:T(8,128)S(1)}, u32[]{:S(2)}, u32[]{:S(2)}) collective-permute-start(f32[26,192]{0,1:T(8,128)S(1)} %slice.149), channel_id=1, source_target_pairs={{0,2},{2,4},{4,6},{6,8},{8,10},{10,12},{12,14},{14,16},{16,18},{18... | collective-permute-start | bytes 59912 | tf_op jit(solution)/shard_map/ppermute | solution.py:330
  44.6 1.7 %collective-permute-start.11 = (f32[26,192]{1,0:T(8,128)S(1)}, f32[26,192]{1,0:T(8,128)S(1)}, u32[]{:S(2)}, u32[]{:S(2)}) collective-permute-start(f32[26,192]{1,0:T(8,128)S(1)} %get-tuple-element.83), channel_id=1, source_target_pairs={{0,30},{2,0},{4,2},{6,4},{8,6},{10,8},{12,10},{14,12},{16,14},{18,... | collective-permute-start | bytes 59912 | tf_op jit(solution)/shard_map/ppermute | solution.py:330
  46.4 3.7 %collective-permute-start.12 = (f32[6,192]{1,0:T(8,128)S(1)}, f32[6,192]{1,0:T(8,128)S(1)}, u32[]{:S(2)}, u32[]{:S(2)}) collective-permute-start(f32[6,192]{1,0:T(8,128)S(1)} %slice_bitcast_fusion.2), channel_id=1, source_target_pairs={{0,1},{1,0},{2,3},{3,2},{4,5},{5,4},{6,7},{7,6},{8,9},{9,8},{10,11... | collective-permute-start | bytes 13832 | tf_op jit(solution)/shard_map/ppermute | solution.py:330
  50.3 3.7 %collective-permute-start.13 = (f32[6,192]{1,0:T(8,128)S(1)}, f32[6,192]{1,0:T(8,128)S(1)}, u32[]{:S(2)}, u32[]{:S(2)}) collective-permute-start(f32[6,192]{1,0:T(8,128)S(1)} %get-tuple-element.85), channel_id=1, source_target_pairs={{0,1},{1,0},{2,3},{3,2},{4,5},{5,4},{6,7},{7,6},{8,9},{9,8},{10,11... | collective-permute-start | bytes 13832 | tf_op jit(solution)/shard_map/ppermute | solution.py:330
  56.5 7.3 %all-to-all-start = ((bf16[2,2,6912]{2,1,0:T(2,128)(2,1)}), bf16[2,2,6912]{2,1,0:T(2,128)(2,1)S(1)}, u32[]{:S(2)}, u32[]{:S(2)}) async-start(bf16[2,2,6912]{2,1,0:T(2,128)(2,1)} %reshape.694), calls=%async_computation | async-start | bytes 110592 | tf_op jit(solution)/shard_map/all_to_all | solution.py:385
  65.5 12.5 %all-to-all-start.1 = ((f32[6,48,96]{2,0,1:T(8,128)}), f32[6,48,96]{2,0,1:T(8,128)S(1)}, u32[]{:S(2)}, u32[]{:S(2)}) async-start(f32[6,48,96]{2,0,1:T(8,128)} %copy.51), calls=%async_computation.1 | async-start | bytes 393216 | tf_op jit(solution)/shard_map/all_to_all | solution.py:389
  80.4 22.2 %all-to-all-start.2 = ((f32[96,3,96]{2,1,0:T(4,128)}), f32[96,3,96]{2,1,0:T(4,128)S(1)}, u32[]{:S(2)}, u32[]{:S(2)}) async-start(f32[96,3,96]{2,1,0:T(4,128)} %copy.56), calls=%async_computation.2 | async-start | bytes 393216 | tf_op jit(solution)/shard_map/all_to_all | solution.py:400
  101.8 0.7 copy-start.3
  102.5 18.1 %collective-permute-start.7 = (bf16[64,512]{1,0:T(8,128)(2,1)S(1)}, bf16[64,512]{1,0:T(8,128)(2,1)S(1)}, u32[]{:S(2)}, u32[]{:S(2)}) collective-permute-start(bf16[64,512]{1,0:T(8,128)(2,1)S(1)} %get-tuple-element.79), channel_id=1, source_target_pairs={{1,0},{0,1},{3,2},{2,3},{5,4},{4,5},{7,6},{6,7},{9,8},{8,9},{11,10... | collective-permute-start | bytes 196616 | tf_op jit(solution)/shard_map/ppermute | solution.py:42
  103.9 19.6 %all-to-all-start.3 = ((f32[6,48,96]{2,0,1:T(8,128)}), f32[6,48,96]{2,0,1:T(8,128)S(1)}, u32[]{:S(2)}, u32[]{:S(2)}) async-start(f32[6,48,96]{2,0,1:T(8,128)} %copy.59), calls=%async_computation.3 | async-start | bytes 393216 | tf_op jit(solution)/shard_map/all_to_all | solution.py:402
  107.3 7.1 %collective-permute-start.5 = (bf16[32,512]{1,0:T(8,128)(2,1)S(1)}, bf16[32,512]{1,0:T(8,128)(2,1)S(1)}, u32[]{:S(2)}, u32[]{:S(2)}) collective-permute-start(bf16[32,512]{1,0:T(8,128)(2,1)S(1)} %get-tuple-element.77), channel_id=1, source_target_pairs={{3,0},{2,1},{5,2},{4,3},{7,4},{6,5},{9,6},{8,7},{11,8},{10,9},{13,... | collective-permute-start | bytes 98312 | tf_op jit(solution)/shard_map/ppermute | solution.py:42
  112.9 2.4 %collective-permute-start.6 = (bf16[32,512]{1,0:T(8,128)(2,1)S(1)}, bf16[32,512]{1,0:T(8,128)(2,1)S(1)}, u32[]{:S(2)}, u32[]{:S(2)}) collective-permute-start(bf16[32,512]{1,0:T(8,128)(2,1)S(1)} %get-tuple-element.78), channel_id=1, source_target_pairs={{2,0},{3,1},{4,2},{5,3},{6,4},{7,5},{8,6},{9,7},{10,8},{11,9},{12,... | collective-permute-start | bytes 98312 | tf_op jit(solution)/shard_map/ppermute | solution.py:42
  113.7 6.9 %collective-permute-start.8 = (bf16[32,512]{1,0:T(8,128)(2,1)S(1)}, bf16[32,512]{1,0:T(8,128)(2,1)S(1)}, u32[]{:S(2)}, u32[]{:S(2)}) collective-permute-start(bf16[32,512]{1,0:T(8,128)(2,1)S(1)} %get-tuple-element.80), channel_id=1, source_target_pairs={{31,0},{30,1},{1,2},{0,3},{3,4},{2,5},{5,6},{4,7},{7,8},{6,9},{9,1... | collective-permute-start | bytes 98312 | tf_op jit(solution)/shard_map/ppermute | solution.py:42
  113.7 6.9 %collective-permute-start.9 = (bf16[32,512]{1,0:T(8,128)(2,1)S(1)}, bf16[32,512]{1,0:T(8,128)(2,1)S(1)}, u32[]{:S(2)}, u32[]{:S(2)}) collective-permute-start(bf16[32,512]{1,0:T(8,128)(2,1)S(1)} %get-tuple-element.81), channel_id=1, source_target_pairs={{30,0},{31,1},{0,2},{1,3},{2,4},{3,5},{4,6},{5,7},{6,8},{7,9},{8,1... | collective-permute-start | bytes 98312 | tf_op jit(solution)/shard_map/ppermute | solution.py:42
  114.5 6.2 %copy-start.14 = (bf16[32,512]{1,0:T(8,128)(2,1)}, bf16[32,512]{1,0:T(8,128)(2,1)S(1)}, u32[]{:S(2)}) copy-start(bf16[32,512]{1,0:T(8,128)(2,1)S(1)} %collective-permute-done.5.rest_0_) | copy-start | bytes 98308
  115.3 5.4 %copy-start.15 = (bf16[32,512]{1,0:T(8,128)(2,1)}, bf16[32,512]{1,0:T(8,128)(2,1)S(1)}, u32[]{:S(2)}) copy-start(bf16[32,512]{1,0:T(8,128)(2,1)S(1)} %collective-permute-done.6.rest_1_) | copy-start | bytes 98308
  120.6 0.6 copy-start.16
  120.6 0.6 copy-start.17
  120.6 0.6 copy-start.12
where the time goes:
time: 126 us
  Pallas kernels  44.6 us (35%)
  waiting for transfers between devices  33.9 us (27%)
  starting transfers between devices  30.5 us (24%)
  local copies, waits for them, and re-layouts  9.45 us (7%)
  matrix products  5.33 us (4%)
    pallas_call x1, Pallas kernels, per_device(): pl.pallas_call(functools.partial(forward_kernel, groups), grid=(slots //...  21 us
    pallas_call x1, Pallas kernels, per_device(): pl.pallas_call(functools.partial(backward_kernel, groups), grid=(slots //...  17.7 us
    ppermute x10, starting transfers between devices, shifted(): return lax.ppermute(value, ('brick', 'pme'), pairs)  15.3 us
    ppermute x4, waiting for transfers between devices, passed_along(): return lax.ppermute(value, axis, pairs)  14 us
    all_to_all x1, waiting for transfers between devices, solve_potential(): lax.all_to_all(spectrum, 'brick', split_axis=1, concat_axis=0, tiled=True)  8.89 us
    ppermute x10, waiting for transfers between devices, shifted(): return lax.ppermute(value, ('brick', 'pme'), pairs)  6.94 us
    unnamed x42, local copies, waits for them, and re-layouts  4.64 us
    all_to_all x1, waiting for transfers between devices, solve_potential(): lax.all_to_all(for_sending(spectrum), 'pme', split_axis=2, concat_axis=1,...  4.04 us
  transfers between devices with their start and end apart: 18, of which 9 were waited for; matrix products, arithmetic and copies ran while one was open for 2% of the time, Pallas kernels for 17%

commit v1 on v0

v1 whole, which is shorter than its diff:
```python
import functools
import itertools
import math

import jax
import jax.numpy as jnp
import ml_dtypes
import numpy as np
from jax import lax
from jax.experimental import pallas as pl
from jax.experimental.pallas import tpu as pltpu
from jax.sharding import PartitionSpec as P

GX = 6
GY = 24
NGZ = 192

CUTOFF = 5.0
SMEAR = 1.0
COUPLING = 0.1
PRECISE = lax.Precision.HIGHEST
BORDER = ((0, 0), (0, 1), (0, 2), (0, 3), (1, 0), (1, 3), (2, 0), (2, 3), (3, 0), (3, 1), (3, 2), (3, 3))
SHIFT = (-1, 0, 0, 1)
QUARTER = (1, 0, 1, 0)
SLOT_BLOCK = 4
WORK = jnp.bfloat16
ROW_GROUP = 16
PIECE = 128
VMEM_LIMIT = 48 * 1024 * 1024


def halo_groups(brick_count, pme_count):
    groups = {}
    for cell, (row, col) in enumerate(BORDER):
        step = (SHIFT[row] % brick_count, SHIFT[col] % pme_count)
        groups.setdefault(step, []).append(cell)
    return tuple((step, tuple(cells)) for step, cells in groups.items())


def shifted(value, brick_step, pme_step):
    bricks, pmes = lax.axis_size("brick"), lax.axis_size("pme")
    pairs = []
    for b in range(bricks):
        for p in range(pmes):
            source = (b + brick_step) % bricks * pmes + (p + pme_step) % pmes
            pairs.append((source, b * pmes + p))
    return lax.ppermute(value, ("brick", "pme"), pairs)


def dot_t(left, right, dims, precision=None):
    return lax.dot_general(
        left, right, (dims, ((), ())), precision=precision, preferred_element_type=jnp.float32
    )


def dot_f32(left, right, dims=((1,), (0,))):
    return dot_t(left, right, dims, PRECISE)


def params(**kwargs):
    return pltpu.CompilerParams(vmem_limit_bytes=VMEM_LIMIT, **kwargs)


def pack_kernel(groups, quad_ref, features_ref, *message_refs):
    atoms = features_ref.shape[0]
    ghost = quad_ref.shape[3]
    rows = lax.broadcasted_iota(jnp.int32, (atoms, ghost), 0)
    picked = {}
    for row in range(2):
        for col in range(2):
            chosen = (rows == quad_ref[0, row, col : col + 1, :]).astype(jnp.bfloat16)
            picked[row, col] = dot_t(chosen, features_ref[...], ((0,), (0,))).astype(jnp.bfloat16)
    for (_, cells), message_ref in zip(groups, message_refs):
        for place, cell in enumerate(cells):
            row, col = BORDER[cell]
            message_ref[place * ghost : (place + 1) * ghost, :] = picked[QUARTER[row], QUARTER[col]]


def radial_kernel(
    vector_ref,
    count_ref,
    basis_weight_ref,
    weight_radial_ref,
    features_ref,
    hidden_ref,
    unit_ref,
    weight_t_ref,
    features_t_ref,
    basis_ref,
):
    load_radial_weight(weight_radial_ref, weight_t_ref)
    transpose_into(features_t_ref, features_ref)
    slots, atoms = vector_ref.shape[1:]
    orders = basis_weight_ref.shape[0]
    parts = [vector_ref[axis] for axis in range(3)]
    distance = jnp.sqrt(parts[0] * parts[0] + parts[1] * parts[1] + parts[2] * parts[2])
    inverse = 1.0 / distance
    for axis in range(3):
        unit_ref[axis] = parts[axis] * inverse
    theta = distance * (math.pi / CUTOFF)
    cosine = jnp.cos(theta)
    live = lax.broadcasted_iota(jnp.int32, (slots, atoms), 0) < count_ref[...]
    envelope = jnp.where(live, 0.5 * (cosine + 1.0), 0.0)
    before = jnp.zeros_like(theta)
    current = jnp.sin(theta) * envelope
    for order in range(orders):
        for slot in range(slots):
            basis_ref[order : order + 1, slot * atoms : (slot + 1) * atoms] = current[slot : slot + 1, :]
        before, current = current, 2.0 * cosine * current - before
    width = 8 * atoms
    for start in range(0, slots * atoms, width):
        inner = dot_f32(basis_weight_ref[...], basis_ref[:, start : start + width], ((0,), (0,)))
        hidden_ref[:, start : start + width] = (inner * jax.nn.sigmoid(inner)).astype(jnp.bfloat16)


def load_radial_weight(weight_ref, weight_t_ref):
    channels = weight_ref.shape[1] // 7
    for path in range(7):
        block = weight_ref[:, path * channels : (path + 1) * channels].astype(jnp.float32)
        if path == 3:
            block = block - weight_ref[:, 4 * channels : 5 * channels].astype(jnp.float32) * (1.0 / 3.0)
        weight_t_ref[path * channels : (path + 1) * channels, :] = block.T.astype(jnp.bfloat16)


def transpose_into(out_ref, rows_ref):
    for lower in range(0, out_ref.shape[0], 128):
        out_ref[lower : lower + 128, :] = (
            rows_ref[:, lower : lower + 128].astype(jnp.float32).T.astype(jnp.bfloat16)
        )


def sender_onehot(index_ref, first, slots, table_rows):
    rows = lax.broadcasted_iota(jnp.int32, (table_rows, index_ref.shape[1]), 0)
    return jnp.concatenate(
        [(rows == index_ref[pl.ds(first + slot, 1), :]).astype(jnp.bfloat16) for slot in range(slots)], axis=1
    )


def unit_rows(unit_ref, first, slot):
    shape = (ROW_GROUP, unit_ref.shape[2])
    rows = [unit_ref[axis, pl.ds(first + slot, 1), :] for axis in range(3)]
    return [jnp.broadcast_to(row, shape).astype(WORK) for row in rows]


def tree_sum(terms):
    while len(terms) > 1:
        terms = [sum(terms[i + 1 : i + 2], terms[i]) for i in range(0, len(terms), 2)]
    return terms[0]


def radial_rows(radial_ref, weight_t_ref, hidden_ref, first, slots, atoms):
    for lower in range(0, slots, 2):
        lanes = pl.ds(pl.multiple_of((first + lower) * atoms, 2 * atoms), 2 * atoms)
        hidden = hidden_ref[:, lanes]
        for row in range(0, radial_ref.shape[0], PIECE):
            radial_ref[row : row + PIECE, lower * atoms : (lower + 2) * atoms] = dot_t(
                weight_t_ref[row : row + PIECE, :], hidden, ((1,), (0,))
            ).astype(WORK)
            yield


def interleave(vector_steps, matrix_steps):
    vector_steps, matrix_steps = iter(vector_steps), iter(matrix_steps)
    done = object()
    going = True
    while going:
        going = next(vector_steps, done) is not done
        for _ in range(3):
            going = (next(matrix_steps, done) is not done) or going


def layer_kernel(
    groups,
    hidden_ref,
    unit_ref,
    index_ref,
    weight_t_ref,
    features_t_ref,
    features_ref,
    weight_scalar_ref,
    weight_gate_ref,
    weight_vector_ref,
    weight_tensor_ref,
    weight_charge_ref,
    cotangent_ref,
    grid_base_ref,
    grid_frac_ref,
    *rest,
):
    count = len(groups)
    message_refs = rest[:count]
    updated_ref, charge_ref, own_grad_ref, *back_refs = rest[count : 2 * count + 3]
    (
        ghosts_ref,
        table_t_ref,
        chosen_ref,
        radial_even,
        radial_odd,
        sender_a,
        sender_b,
        total_ref,
        node_grad_ref,
        grad_a,
        grad_b,
        table_grad_ref,
    ) = rest[2 * count + 3 :]
    atoms, width = features_ref.shape
    channels = width // 4
    ghost = ghosts_ref.shape[0] // 12
    table_rows = table_t_ref.shape[1]
    slots = SLOT_BLOCK
    blocks = index_ref.shape[0] // slots
    steps = blocks // 2

    def products(block, radial_ref, sender_ref):
        first = block * slots
        yield from radial_rows(radial_ref, weight_t_ref, hidden_ref, first, slots, atoms)
        for lower in range(0, slots, 2):
            chosen = sender_onehot(index_ref, first + lower, 2, table_rows)
            chosen_ref[block, :, lower * atoms : (lower + 2) * atoms] = chosen
            for row in range(0, width, PIECE):
                sender_ref[row : row + PIECE, lower * atoms : (lower + 2) * atoms] = dot_t(
                    table_t_ref[row : row + PIECE, :], chosen, ((1,), (0,))
                ).astype(WORK)
                yield

    def messages(block, radial_ref, sender_ref):
        first = block * slots
        units = [unit_rows(unit_ref, first, slot) for slot in range(slots)]
        for row in range(0, channels, ROW_GROUP):
            terms = [[] for _ in range(10)]
            for slot in range(slots):
                lanes = slice(slot * atoms, (slot + 1) * atoms)
                unit = units[slot]
                paths = [
                    radial_ref[path * channels + row : path * channels + row + ROW_GROUP, lanes]
                    for path in range(7)
                ]
                scalar, *vector = [
                    sender_ref[part * channels + row : part * channels + row + ROW_GROUP, lanes]
                    for part in range(4)
                ]
                along = unit[0] * vector[0] + unit[1] * vector[1] + unit[2] * vector[2]
                terms[0].append(paths[0] * scalar + paths[1] * along)
                pushed = paths[2] * scalar + paths[4] * along
                twisted = paths[5] * scalar
                mixed = []
                for axis in range(3):
                    terms[1 + axis].append(unit[axis] * pushed + paths[3] * vector[axis])
                    mixed.append(unit[axis] * twisted + paths[6] * vector[axis])
                    terms[4 + axis].append(unit[axis] * mixed[axis])
                for place, (left, right) in enumerate(((0, 1), (1, 2), (0, 2))):
                    terms[7 + place].append(unit[left] * mixed[right] + unit[right] * mixed[left])
            for number in range(10):
                total_ref[number, row : row + ROW_GROUP, :] += tree_sum(terms[number]).astype(jnp.float32)
            yield

    for (_, cells), message_ref in zip(groups, message_refs):
        for place, cell in enumerate(cells):
            ghosts_ref[cell * ghost : (cell + 1) * ghost, :] = message_ref[
                place * ghost : (place + 1) * ghost, :
            ]
    table_t_ref[:, :atoms] = features_t_ref[...]
    transpose_into(table_t_ref.at[:, atoms:], ghosts_ref)
    total_ref[...] = jnp.zeros_like(total_ref)
    for _ in products(0, radial_even.at[0], sender_a):
        pass

    def forward_step(step, carry):
        interleave(
            messages(2 * step, radial_even.at[step], sender_a),
            products(2 * step + 1, radial_odd.at[step], sender_b),
        )
        following = jnp.minimum(2 * step + 2, blocks - 1)
        interleave(
            messages(2 * step + 1, radial_odd.at[step], sender_b),
            products(following, radial_even.at[step + 1], sender_a),
        )
        return carry

    lax.fori_loop(0, steps, forward_step, 0)
    scale = 1.0 / math.sqrt(index_ref.shape[0])
    trace = (total_ref[4] + total_ref[5] + total_ref[6]) * (1.0 / 3.0)
    sums = [total_ref[0], total_ref[1], total_ref[2], total_ref[3]]
    sums += [total_ref[4] - trace, total_ref[5] - trace]
    sums += [0.5 * total_ref[7], 0.5 * total_ref[8], 0.5 * total_ref[9]]
    aggregate = [(block * scale).T for block in sums]
    columns = lambda ref, block: ref[:, block * channels : (block + 1) * channels].astype(jnp.float32)
    gate = jax.nn.sigmoid(dot_f32(aggregate[0], weight_gate_ref[...]))
    inner = dot_f32(aggregate[0], weight_scalar_ref[...])
    inner_sigmoid = jax.nn.sigmoid(inner)
    vectors = dot_f32(jnp.concatenate(aggregate[1:4], axis=0), weight_vector_ref[...])
    tensors = dot_f32(jnp.concatenate(aggregate[4:9], axis=0), weight_tensor_ref[...])
    gate_v, gate_t = gate[:, :channels], gate[:, channels:]
    scalar_out = (columns(features_ref, 0) + inner * inner_sigmoid).astype(jnp.bfloat16)
    updated_ref[:, :channels] = scalar_out
    charge = dot_f32(weight_charge_ref[...], scalar_out.astype(jnp.float32), ((1,), (1,)))
    base, own_lines = grid_base_ref[...], lax.axis_index("pme") * GY
    rows = [charge, base[0:1], base[1:2] + own_lines, base[2:3], grid_frac_ref[...], jnp.zeros_like(charge)]
    rows = jnp.concatenate([row.astype(jnp.float32) for row in rows], axis=0)
    for device in range(charge_ref.shape[0]):
        charge_ref[device] = rows
    grad_v, grad_t = [], []
    gate_grad_v = jnp.zeros((atoms, channels), jnp.float32)
    gate_grad_t = jnp.zeros((atoms, channels), jnp.float32)
    for axis in range(3):
        value = vectors[axis * atoms : (axis + 1) * atoms]
        given = columns(cotangent_ref, 1 + axis)
        updated_ref[:, (1 + axis) * channels : (2 + axis) * channels] = (
            columns(features_ref, 1 + axis) + gate_v * value
        ).astype(jnp.bfloat16)
        gate_grad_v = gate_grad_v + given * value
        grad_v.append(given * gate_v)
    for block in range(5):
        value = tensors[block * atoms : (block + 1) * atoms]
        given = columns(cotangent_ref, 4 + block)
        updated_ref[:, (4 + block) * channels : (5 + block) * channels] = (gate_t * value).astype(
            jnp.bfloat16
        )
        gate_grad_t = gate_grad_t + given * value
        grad_t.append(given * gate_t)
    inner_grad = columns(cotangent_ref, 0) * (
        inner_sigmoid * (1.0 + inner * (1.0 - inner_sigmoid))
    )
    gate_grad = jnp.concatenate([gate_grad_v, gate_grad_t], axis=1) * (gate * (1.0 - gate))
    across = ((1,), (1,))
    grad_s = dot_f32(inner_grad, weight_scalar_ref[...], across)
    grad_s = grad_s + dot_f32(gate_grad, weight_gate_ref[...], across)
    grad_v = dot_f32(jnp.concatenate(grad_v, axis=0), weight_vector_ref[...], across)
    grad_t = dot_f32(jnp.concatenate(grad_t, axis=0), weight_tensor_ref[...], across)
    t00, t11, t01, t12, t02 = [grad_t[block * atoms : (block + 1) * atoms] for block in range(5)]
    third = (t00 + t11) * (1.0 / 3.0)
    pieces = [grad_s] + [grad_v[axis * atoms : (axis + 1) * atoms] for axis in range(3)]
    pieces += [t00 - third, t11 - third, -third, 0.5 * t01, 0.5 * t12, 0.5 * t02]
    for block in range(10):
        node_grad_ref[block] = (pieces[block] * scale).T


    table_grad_ref[...] = jnp.zeros_like(table_grad_ref)
    grad_b[...] = jnp.zeros_like(grad_b)

    def collect(block, grad_ref):
        for lower in range(0, width, 2 * channels):
            table_grad_ref[:, lower : lower + 2 * channels] += dot_t(
                chosen_ref[block], grad_ref[lower : lower + 2 * channels, :], ((1,), (1,))
            )
            yield

    def gradients(block, radial_ref, grad_ref):
        first = block * slots
        units = [unit_rows(unit_ref, first, slot) for slot in range(slots)]
        for row in range(0, channels, ROW_GROUP):
            node = [node_grad_ref[number, row : row + ROW_GROUP, :].astype(WORK) for number in range(10)]
            g_s, g_v, diag = node[0], node[1:4], node[4:7]
            off_01, off_12, off_02 = node[7:10]
            for slot in range(slots):
                lanes = slice(slot * atoms, (slot + 1) * atoms)
                unit = units[slot]
                paths = [
                    radial_ref[path * channels + row : path * channels + row + ROW_GROUP, lanes]
                    for path in range(7)
                ]
                along = unit[0] * g_v[0] + unit[1] * g_v[1] + unit[2] * g_v[2]
                bent = [
                    unit[0] * diag[0] + unit[1] * off_01 + unit[2] * off_02,
                    unit[0] * off_01 + unit[1] * diag[1] + unit[2] * off_12,
                    unit[0] * off_02 + unit[1] * off_12 + unit[2] * diag[2],
                ]
                twice = unit[0] * bent[0] + unit[1] * bent[1] + unit[2] * bent[2]
                pushed = paths[1] * g_s + paths[4] * along
                parts = [paths[0] * g_s + paths[2] * along + paths[5] * twice]
                for axis in range(3):
                    parts.append(unit[axis] * pushed + paths[3] * g_v[axis] + paths[6] * bent[axis])
                for number, part in enumerate(parts):
                    lower = number * channels + row
                    grad_ref[lower : lower + ROW_GROUP, lanes] = part.astype(jnp.bfloat16)
            yield

    def backward_step(step, carry):
        before = jnp.maximum(2 * step - 1, 0)
        interleave(gradients(2 * step, radial_even.at[step], grad_a), collect(before, grad_b))
        interleave(gradients(2 * step + 1, radial_odd.at[step], grad_b), collect(2 * step, grad_a))
        return carry

    lax.fori_loop(0, steps, backward_step, 0)
    for _ in collect(blocks - 1, grad_b):
        pass
    own_grad_ref[...] = table_grad_ref[:atoms, :] + cotangent_ref[:, :width].astype(jnp.float32)
    for (_, cells), back_ref in zip(groups, back_refs):
        for place, cell in enumerate(cells):
            lower = atoms + cell * ghost
            back_ref[place * ghost : (place + 1) * ghost, :] = table_grad_ref[
                lower : lower + ghost, :
            ].astype(jnp.bfloat16)


def gather_kernel(groups, quad_ref, own_ref, _, *rest):
    message_refs, out_ref = rest[: len(groups)], rest[len(groups)]
    atoms = own_ref.shape[0]
    ghost = quad_ref.shape[3]
    rows = lax.broadcasted_iota(jnp.int32, (atoms, ghost), 0)
    total = own_ref[...]
    for (_, cells), message_ref in zip(groups, message_refs):
        for place, cell in enumerate(cells):
            row, col = QUARTER[BORDER[cell][0]], QUARTER[BORDER[cell][1]]
            chosen = (rows == quad_ref[0, row, col : col + 1, :]).astype(jnp.bfloat16)
            total = total + dot_t(chosen, message_ref[place * ghost : (place + 1) * ghost, :], ((1,), (0,)))
    out_ref[...] = total


def whole(shape):
    return pl.BlockSpec(shape, lambda step: (0,) * len(shape))


def split_f32(value):
    high = value.astype(jnp.bfloat16)
    return high, (value - high.astype(jnp.float32)).astype(jnp.bfloat16)


def split_np(value):
    high = value.astype(ml_dtypes.bfloat16)
    low = (value - high.astype(np.float64)).astype(ml_dtypes.bfloat16)
    return np.concatenate([high, low], axis=0)


def hartley_np(points):
    angle = 2.0 * np.pi / points * (np.outer(np.arange(points), np.arange(points)) % points)
    return np.cos(angle) + np.sin(angle)


def damping_np(points):
    index = np.arange(points)
    folded = np.minimum(index, points - index) / points
    modulus = 0.75 + 0.25 * np.cos(2.0 * np.pi / points * index)
    return folded**2, np.exp(-2.0 * np.pi**2 * SMEAR**2 * folded**2) / modulus**2


def grid_tables(bricks, cells_x, cells_y, full_y, cells_z):
    full_x = bricks * cells_x
    wave_x, wave_y, wave_z = hartley_np(full_x), hartley_np(full_y), hartley_np(cells_z)
    (square_x, damp_x), (_, damp_y), (square_z, damp_z) = map(damping_np, (full_x, full_y, cells_z))
    window = (np.arange(bricks)[:, None] * cells_x + np.arange(-1, cells_x + 1)[None, :]) % full_x
    own_x = np.zeros((bricks, cells_x + 2, full_x))
    own_x[:, :cells_x] = (wave_x * damp_x[None, :]).reshape(bricks, cells_x, full_x)
    own_x = np.concatenate([split_np(block) for block in own_x], axis=0)
    scale = COUPLING / (full_x * full_y * cells_z)
    return (
        split_np(wave_z),
        split_np(wave_y),
        split_np(wave_x[:, window.reshape(-1)]),
        own_x,
        (wave_y * damp_y[None, :]).astype(np.float32),
        (wave_z * damp_z[:, None] * scale).astype(np.float32),
        square_x.reshape(-1, 1).astype(np.float32),
        square_z.reshape(1, -1).astype(np.float32),
    )


def spline_rows(cells, base, offset, points):
    weights = (
        0.5 * (0.5 - offset) * (0.5 - offset),
        0.75 - offset * offset,
        0.5 * (0.5 + offset) * (0.5 + offset),
    )
    below, above = base - 1.0, base + 1.0
    if points:
        below = jnp.where(below < 0.0, below + points, below)
        above = jnp.where(above >= points, above - points, above)
    table = jnp.where(cells == above, weights[2], 0.0)
    table = jnp.where(cells == below, weights[0], table)
    return jnp.where(cells == base, weights[1], table)


def dot_split(left, right, dims=((1,), (0,))):
    rows = left.shape[0] // 2
    both = dot_t(left, right[0], dims)
    return both[:rows] + both[rows:] + dot_t(left[:rows], right[1], dims)


def cell_numbers(rows, lanes):
    return lax.broadcasted_iota(jnp.int32, (rows, lanes), 0).astype(jnp.float32)


def potential_kernel(
    cells_y,
    atoms_ref,
    wave_z_ref,
    wave_y_ref,
    wave_x_ref,
    own_x_ref,
    own_y_ref,
    own_z_ref,
    square_x_ref,
    square_z_ref,
    out_ref,
    shape_z_ref,
    lines_ref,
    square_ref,
    planes_ref,
):
    step = pl.program_id(0)
    bricks, pieces, _, piece_atoms = atoms_ref.shape
    atoms = pieces * piece_atoms
    cells_x, _, cells_z = out_ref.shape
    window = cells_x + 2
    full_y = planes_ref.shape[0]
    chunk = lines_ref.shape[0]

    @pl.when(step == 0)
    def _():
        square_ref[...] = square_x_ref[...] + square_z_ref[...]

        def tables(brick, carry):
            block = jnp.concatenate([atoms_ref[brick, piece] for piece in range(pieces)], axis=1)
            row = lambda number: block[number : number + 1, :]
            table = spline_rows(cell_numbers(cells_z, atoms), row(3), row(6), float(cells_z))
            high, low = split_f32(dot_split(wave_z_ref[...], split_f32(table)))
            shape_z_ref[brick, 0], shape_z_ref[brick, 1] = high, low
            return carry

        lax.fori_loop(0, bricks, tables, 0, unroll=4)

    first = step * chunk

    def spread(brick, carry):
        block = jnp.concatenate([atoms_ref[brick, piece] for piece in range(pieces)], axis=1)
        row = lambda number: block[number : number + 1, :]
        along_x = row(0) * spline_rows(cell_numbers(window, atoms) - 1.0, row(1), row(4), 0)
        table = spline_rows(cell_numbers(full_y, atoms), row(2), row(5), float(full_y))
        wave_y = jnp.concatenate(
            [wave_y_ref[pl.ds(pl.multiple_of(first + part, 16), chunk), :] for part in (0, full_y)], axis=0
        )
        along_y = dot_split(wave_y, split_f32(table))
        rows = jnp.concatenate([along_y[line : line + 1, :] * along_x for line in range(chunk)], axis=0)
        high, low = split_f32(rows)
        z_high, z_low = shape_z_ref[brick, 0], shape_z_ref[brick, 1]
        across = ((1,), (1,))
        grid = dot_t(high, z_high, across) + dot_t(high, z_low, across) + dot_t(low, z_high, across)
        lines_ref[:, pl.ds(pl.multiple_of(brick * window, window), window), :] = grid.reshape(
            chunk, window, cells_z
        )
        return carry

    lax.fori_loop(0, bricks, spread, 0, unroll=2)
    own = pl.multiple_of(lax.axis_index("brick") * (2 * window), 2 * window)

    def solve(line, carry):
        wave = dot_split(wave_x_ref[...], split_f32(lines_ref[line]))
        number = first + line
        height = jnp.minimum(number, full_y - number).astype(jnp.float32) * (1.0 / full_y)
        square = square_ref[...] + height * height
        wave = wave * jnp.where(square > 0.0, 1.0 / jnp.where(square > 0.0, square, 1.0), 0.0)
        planes_ref[number] = dot_split(own_x_ref[pl.ds(own, 2 * window), :], split_f32(wave))
        return carry

    lax.fori_loop(0, chunk, solve, 0, unroll=8)

    @pl.when(step == pl.num_programs(0) - 1)
    def _():
        along_y = own_y_ref[pl.ds(pl.multiple_of(lax.axis_index("pme") * cells_y, 8), cells_y), :]
        for plane in range(cells_x):
            lines = dot_f32(along_y, planes_ref[:, plane, :])
            out_ref[plane] = dot_f32(lines, own_z_ref[...])


def potential_block(gathered, cells_x, cells_y, cells_z):
    bricks, pieces, rows, piece_atoms = gathered.shape
    full_y = cells_y * pieces
    atoms = pieces * piece_atoms
    window = cells_x + 2
    tables = grid_tables(bricks, cells_x, cells_y, full_y, cells_z)
    chunk = full_y if full_y <= 48 else 16
    return pl.pallas_call(
        functools.partial(potential_kernel, cells_y),
        grid=(full_y // chunk,),
        in_specs=[whole(gathered.shape)] + [whole(table.shape) for table in tables],
        out_specs=whole((cells_x, cells_y, cells_z)),
        out_shape=jax.ShapeDtypeStruct((cells_x, cells_y, cells_z), jnp.float32),
        scratch_shapes=[
            pltpu.VMEM((bricks, 2, cells_z, atoms), jnp.bfloat16),
            pltpu.VMEM((chunk, bricks * window, cells_z), jnp.float32),
            pltpu.VMEM((bricks * cells_x, cells_z), jnp.float32),
            pltpu.VMEM((full_y, window, cells_z), jnp.float32),
        ],
        compiler_params=params(),
        cost_estimate=pl.CostEstimate(flops=2 * 10**10, bytes_accessed=10**7, transcendentals=0),
        name="potential",
    )(gathered, *[jnp.asarray(table) for table in tables])


def all_charges(copies):
    bricks, pmes = lax.axis_size("brick"), lax.axis_size("pme")
    arrived = lax.all_to_all(copies, ("brick", "pme"), split_axis=0, concat_axis=0, tiled=True)
    return arrived.reshape(bricks, pmes, *copies.shape[1:])


def per_device(
    features,
    cotangent,
    neighbor_index,
    neighbor_count,
    edge_vector,
    quad_index,
    weight_basis,
    weight_radial,
    weight_scalar,
    weight_gate,
    weight_vector,
    weight_tensor,
    weight_charge,
    grid_base,
    grid_frac,
):
    atoms, width = features.shape
    channels = width // 4
    slots = neighbor_index.shape[0] // atoms
    ghost = quad_index.shape[3]
    table_rows = atoms + 12 * ghost
    hidden_units = weight_basis.shape[1]
    groups = halo_groups(lax.axis_size("brick"), lax.axis_size("pme"))
    message_shapes = [
        jax.ShapeDtypeStruct((len(cells) * ghost, width), jnp.bfloat16) for _, cells in groups
    ]

    outgoing = pl.pallas_call(
        functools.partial(pack_kernel, groups), out_shape=message_shapes, name="pack"
    )(quad_index, features)
    incoming = [shifted(value, *steps) for (steps, _), value in zip(groups, outgoing)]

    index_t = neighbor_index.reshape(atoms, slots).T
    vector_t = edge_vector.reshape(3, atoms, slots).transpose(0, 2, 1)
    hidden, unit, weight_t, features_t = pl.pallas_call(
        radial_kernel,
        out_shape=[
            jax.ShapeDtypeStruct((hidden_units, slots * atoms), jnp.bfloat16),
            jax.ShapeDtypeStruct((3, slots, atoms), jnp.float32),
            jax.ShapeDtypeStruct((7 * channels, hidden_units), jnp.bfloat16),
            jax.ShapeDtypeStruct((width, atoms), jnp.bfloat16),
        ],
        scratch_shapes=[pltpu.VMEM((weight_basis.shape[0], slots * atoms), jnp.float32)],
        compiler_params=params(),
        name="radial",
    )(vector_t, neighbor_count.reshape(1, atoms), weight_basis, weight_radial, features)

    block = SLOT_BLOCK * atoms
    steps = slots // (2 * SLOT_BLOCK)
    devices = lax.axis_size("brick") * lax.axis_size("pme")
    updated, charges, own_grad, *ghost_grads = pl.pallas_call(
        functools.partial(layer_kernel, groups),
        out_shape=[
            jax.ShapeDtypeStruct((atoms, 9 * channels), jnp.bfloat16),
            jax.ShapeDtypeStruct((devices, 8, atoms), jnp.float32),
            jax.ShapeDtypeStruct((atoms, width), jnp.float32),
        ]
        + message_shapes,
        scratch_shapes=[
            pltpu.VMEM((12 * ghost, width), jnp.bfloat16),
            pltpu.VMEM((width, table_rows), jnp.bfloat16),
            pltpu.VMEM((2 * steps, table_rows, block), jnp.bfloat16),
            pltpu.VMEM((steps + 1, 7 * channels, block), WORK),
            pltpu.VMEM((steps, 7 * channels, block), WORK),
            pltpu.VMEM((width, block), WORK),
            pltpu.VMEM((width, block), WORK),
            pltpu.VMEM((10, channels, atoms), jnp.float32),
            pltpu.VMEM((10, channels, atoms), jnp.float32),
            pltpu.VMEM((width, block), jnp.bfloat16),
            pltpu.VMEM((width, block), jnp.bfloat16),
            pltpu.VMEM((table_rows, width), jnp.float32),
        ],
        compiler_params=params(),
        name="layer",
    )(
        hidden,
        unit,
        index_t,
        weight_t,
        features_t,
        features,
        weight_scalar,
        weight_gate,
        weight_vector,
        weight_tensor,
        weight_charge.reshape(1, channels),
        cotangent,
        grid_base,
        grid_frac,
        *incoming,
    )
    gathered = all_charges(charges)
    potential = potential_block(gathered, GX, GY, NGZ)
    returned = [shifted(value, -steps[0], -steps[1]) for (steps, _), value in zip(groups, ghost_grads)]
    feature_grad = pl.pallas_call(
        functools.partial(gather_kernel, groups),
        in_specs=[pl.BlockSpec(memory_space=pltpu.VMEM)] * 2
        + [pl.BlockSpec(memory_space=pl.ANY)]
        + [pl.BlockSpec(memory_space=pltpu.VMEM)] * len(groups),
        out_shape=jax.ShapeDtypeStruct((atoms, width), jnp.float32),
        name="gather",
    )(quad_index, own_grad, potential, *returned)

    return (updated, feature_grad, potential)


def solution(mesh):
    placed = (
        P(("brick", "pme"), None),
        P(("brick", "pme"), None),
        P(("brick", "pme")),
        P(("brick", "pme")),
        P(None, ("brick", "pme")),
        P(("brick", "pme"), None, None, None),
        P(),
        P(),
        P(),
        P(),
        P(),
        P(),
        P(),
        P(None, ("brick", "pme")),
        P(None, ("brick", "pme")),
    )
    return jax.shard_map(
        per_device,
        mesh=mesh,
        in_specs=placed,
        out_specs=(P(("brick", "pme"), None), P(("brick", "pme"), None), P("brick", "pme", None)),
        check_vma=False,
    )
```

time: 126 us -> 75.4 us (0.60)
  waiting for transfers between devices: 33.9 us -> 1.33 us
  starting transfers between devices: 30.5 us -> 20 us
  local copies, waits for them, and re-layouts: 9.45 us -> 3.24 us
  matrix products: 5.33 us -> 0 us
  Pallas kernels: 44.6 us -> 49.6 us
    ppermute x4 -> x0, waiting for transfers between devices: 14 us -> none  [passed_along(): return lax.ppermute(value, axis, pairs)]
    all_to_all x4 -> x1, waiting for transfers between devices: 12.9 us -> 1.3 us  [all_charges(): lax.all_to_all(copies, ('brick', 'pme'), split_axis=0, concat_axis=0, til...]
    all_to_all x4 -> x1, starting transfers between devices: 13.9 us -> 3.63 us  [all_charges(): lax.all_to_all(copies, ('brick', 'pme'), split_axis=0, concat_axis=0, til...]
    ppermute x10, waiting for transfers between devices: 6.94 us -> 0.03 us  [shifted(): return lax.ppermute(value, ('brick', 'pme'), pairs)]
    dot_general x7 -> x0, matrix products: 5.33 us -> none  [the longest x1 1.76 us: solve_potential(): jnp.dot(spectrum.reshape(-1, cells_z), table_z, precision=PRECISE)]
    pallas_call x3, Pallas kernels: 40.9 us -> 45.9 us  [the longest x1 25.8 us: per_device(): pl.pallas_call(functools.partial(layer_kernel, groups), out_shape=[jax.Sh...]
    unnamed x42 -> x56, local copies, waits for them, and re-layouts: 4.64 us -> 2.83 us
    transpose x2 -> x0, local copies, waits for them, and re-layouts: 1.45 us -> none  [solve_potential(): spectrum = jnp.einsum('xyz,yk->xkz', spectrum, table_y, precision=PRECISE)]
  transfers between devices with their start and end apart: 18 -> 11, of which waited for: 9 -> 1; matrix products, arithmetic and copies ran while one was open for 2% -> 1% of each run, Pallas kernels for 17% -> 26%
where the time goes in v1:
time: 75.4 us; the launch traced here: 75.1 us
  Pallas kernels  49.6 us (66%)
  starting transfers between devices  20 us (27%)
  local copies, waits for them, and re-layouts  3.24 us (4%)
  waiting for transfers between devices  1.33 us (2%)
  between operations  0.95 us (1%)
    pallas_call x1, Pallas kernels, per_device(): pl.pallas_call(functools.partial(layer_kernel, groups), out_shape=[jax.Sh...  25.8 us
    pallas_call x1, Pallas kernels, potential_block(): pl.pallas_call(functools.partial(potential_kernel, cells_y), grid=(full_y...  17.8 us
    ppermute x10, starting transfers between devices, shifted(): return lax.ppermute(value, ('brick', 'pme'), pairs)  16.4 us
    all_to_all x1, starting transfers between devices, all_charges(): lax.all_to_all(copies, ('brick', 'pme'), split_axis=0, concat_axis=0, til...  3.63 us
    unnamed x56, local copies, waits for them, and re-layouts  2.83 us
    pallas_call x1, Pallas kernels, per_device(): pl.pallas_call(functools.partial(gather_kernel, groups), in_specs=[pl.Blo...  2.23 us
    pallas_call x1, Pallas kernels, per_device(): pl.pallas_call(radial_kernel, out_shape=[jax.ShapeDtypeStruct((hidden_uni...  1.86 us
    pallas_call x1, Pallas kernels, per_device(): pl.pallas_call(functools.partial(pack_kernel, groups), out_shape=message_...  1.8 us
  transfers between devices with their start and end apart: 11, of which 1 were waited for; matrix products, arithmetic and copies ran while one was open for 1% of the time, Pallas kernels for 26%

profile of v1, /device:TPU:0, one launch (start us, length us, event | category | flops | bytes accessed | tf_op | source)
XLA Modules:
  0.0 75.1 jit_solution(3278735736131903529)
XLA Ops:
  0.6 0.0 copy-start.23
  0.6 1.8 %pack.1 = (bf16[32,512]{1,0:T(8,128)(2,1)}, bf16[32,512]{1,0:T(8,128)(2,1)}, bf16[64,512]{1,0:T(8,128)(2,1)}, bf16[32,512]{1,0:T(8,128)(2,1)}, bf16[32,512]{1,0:T(8,128)(2,1)}) custom-call(s32[1,2,2,16]{3,2,1,0:T(2,128)} %quad_ref.3, bf16[128,512]{1,0:T(8,128)(2,1)} %features_ref.5), custom_call_target="tpu_custom_call" | custom-call | tf_op jit(solution)/shard_map/pack/pallas_call | solution.py:625
  2.4 3.0 %collective-permute-start.2 = (bf16[64,512]{1,0:T(8,128)(2,1)}, bf16[64,512]{1,0:T(8,128)(2,1)S(1)}, u32[]{:S(2)}, u32[]{:S(2)}) collective-permute-start(bf16[64,512]{1,0:T(8,128)(2,1)} %get-tuple-element.26), channel_id=1, source_target_pairs={{1,0},{0,1},{3,2},{2,3},{5,4},{4,5},{7,6},{6,7},{9,8},{8,9},{11,10... | collective-permute-start | bytes 196616 | tf_op jit(solution)/shard_map/ppermute | solution.py:47
  5.4 0.0 collective-permute-start
  5.4 1.5 %collective-permute-start.1 = (bf16[32,512]{1,0:T(8,128)(2,1)}, bf16[32,512]{1,0:T(8,128)(2,1)S(1)}, u32[]{:S(2)}, u32[]{:S(2)}) collective-permute-start(bf16[32,512]{1,0:T(8,128)(2,1)} %get-tuple-element.25), channel_id=1, source_target_pairs={{30,0},{31,1},{0,2},{1,3},{2,4},{3,5},{4,6},{5,7},{6,8},{7,9},{8,1... | collective-permute-start | bytes 98312 | tf_op jit(solution)/shard_map/ppermute | solution.py:47
  7.0 3.8 %collective-permute-start.3 = (bf16[32,512]{1,0:T(8,128)(2,1)}, bf16[32,512]{1,0:T(8,128)(2,1)S(1)}, u32[]{:S(2)}, u32[]{:S(2)}) collective-permute-start(bf16[32,512]{1,0:T(8,128)(2,1)} %get-tuple-element.27), channel_id=1, source_target_pairs={{3,0},{2,1},{5,2},{4,3},{7,4},{6,5},{9,6},{8,7},{11,8},{10,9},{13,... | collective-permute-start | bytes 98312 | tf_op jit(solution)/shard_map/ppermute | solution.py:47
  10.8 0.7 collective-permute-start.4
  11.4 0.0 copy-done.23
  11.4 0.1 reshape.23
  11.5 0.1 copy.27
  11.6 0.0 copy-done.21
  11.6 0.0 copy-start.4
  11.6 0.0 copy-start.8
  11.6 0.0 copy-start.11
  11.6 0.0 copy-start.6
  11.7 0.0 copy-start.7
  11.7 0.2 reshape.21
  11.8 0.1 copy.26
  11.9 0.6 copy-done.4
  12.5 0.0 copy-done.8
  12.5 0.0 copy-done.11
  12.5 0.2 copy-done
  12.7 1.9 %radial.1 = (bf16[64,8192]{1,0:T(8,128)(2,1)S(1)}, f32[3,64,128]{2,1,0:T(8,128)S(1)}, bf16[896,64]{1,0:T(8,128)(2,1)S(1)}, bf16[512,128]{1,0:T(8,128)(2,1)S(1)}) custom-call(f32[3,64,128]{2,1,0:T(8,128)S(1)} %bitcast.5, s32[1,128]{1,0:T(1,128)S(1)} %bitcast.8, f32[8,64]{1,0:T(8,128)S(1)} %copy-done.8, bf16[64,896]{1,0:T(8,128)(2,1)S(1)} %copy-done.4, ...), custom_call_target="tpu_custom_call" | custom-call | tf_op jit(solution)/shard_map/radial/pallas_call | solution.py:632
  14.6 0.0 collective-permute-done.rest_0_
  14.6 0.0 collective-permute-done.1.rest_1_
  14.6 0.0 collective-permute-done.3.rest_3_
  14.6 0.0 collective-permute-done.4.rest_4_
  14.6 0.0 collective-permute-done.2.rest_2_
  14.6 0.0 copy-start.10
  14.7 0.0 copy-start.9
  14.7 0.0 copy-start.12
  14.7 0.0 copy-done.6
  14.7 0.0 copy-done.7
  14.7 0.0 copy-done.1
  14.7 0.0 copy-done.3
  14.7 0.0 copy-done.5
  14.7 0.6 copy-done.10
  15.3 0.0 copy-done.9
  15.3 0.0 copy-done.12
  15.4 0.0 copy-start.18
  15.4 0.0 copy-start.19
  15.4 25.8 %layer.1 = (bf16[128,1152]{1,0:T(8,128)(2,1)}, f32[32,8,128]{2,1,0:T(8,128)}, f32[128,512]{1,0:T(8,128)S(1)}, bf16[32,512]{1,0:T(8,128)(2,1)S(1)}, bf16[32,512]{...) custom-call(bf16[64,8192]{1,0:T(8,128)(2,1)S(1)} %get-tuple-element.20., ...), custom_call_target="tpu_custom_call" | custom-call | tf_op jit(solution)/shard_map/layer/pallas_call | solution.py:648
  41.2 0.7 copy-done.2
  41.9 3.6 %all-to-all-start = ((f32[32,8,128]{2,1,0:T(8,128)}), f32[32,8,128]{2,1,0:T(8,128)S(1)}, u32[]{:S(2)}, u32[]{:S(2)}) async-start(f32[32,8,128]{2,1,0:T(8,128)} %get-tuple-element.31), calls=%async_computation | async-start | bytes 262144 | tf_op jit(solution)/shard_map/all_to_all | solution.py:593
  45.6 5.3 %collective-permute-start.5 = (bf16[32,512]{1,0:T(8,128)(2,1)S(1)}, bf16[32,512]{1,0:T(8,128)(2,1)S(1)}, u32[]{:S(2)}, u32[]{:S(2)}) collective-permute-start(bf16[32,512]{1,0:T(8,128)(2,1)S(1)} %get-tuple-element.32), channel_id=1, source_target_pairs={{3,0},{2,1},{5,2},{4,3},{7,4},{6,5},{9,6},{8,7},{11,8},{10,9},{13,... | collective-permute-start | bytes 98312 | tf_op jit(solution)/shard_map/ppermute | solution.py:47
  50.8 0.5 collective-permute-start.6
  51.4 0.1 collective-permute-start.8
  51.5 0.0 collective-permute-start.9
  51.5 1.5 %collective-permute-start.7 = (bf16[64,512]{1,0:T(8,128)(2,1)S(1)}, bf16[64,512]{1,0:T(8,128)(2,1)S(1)}, u32[]{:S(2)}, u32[]{:S(2)}) collective-permute-start(bf16[64,512]{1,0:T(8,128)(2,1)S(1)} %get-tuple-element.34), channel_id=1, source_target_pairs={{1,0},{0,1},{3,2},{2,3},{5,4},{4,5},{7,6},{6,7},{9,8},{8,9},{11,10... | collective-permute-start | bytes 196616 | tf_op jit(solution)/shard_map/ppermute | solution.py:47
  53.0 1.3 %all-to-all-done = f32[32,8,128]{2,1,0:T(8,128)S(1)} async-done(((f32[32,8,128]{2,1,0:T(8,128)}), f32[32,8,128]{2,1,0:T(8,128)S(1)}, u32[]{:S(2)}, u32[]{:S(2)}) %all-to-all-start) | async-done | bytes 131104 | tf_op jit(solution)/shard_map/all_to_all | solution.py:593
  54.3 0.0 copy-done.14
  54.4 17.8 %potential.1._ = f32[6,24,192]{2,1,0:T(8,128)} custom-call(f32[16,2,8,128]{3,2,1,0:T(8,128)S(1)} %bitcast.7, bf16[384,192]{1,0:T(8,128)(2,1)S(1)} %copy-done.14, bf16[96,48]{1,0:T(8,128)(2,1)S(1)} %copy-done.19, bf16[192,128]{1,0:T(8,128)(2,1)S(1)} %copy-done.17, bf16[256,96]{1,0:T(8,128)(2,1)S(1)} %copy-done.15, f32[48,48]{1,0:T(8,128)S(1)} %copy-done.18, ...), custom_call_target="tpu_custom_call" | custom-call | flops 20000000000 | bytes 10000000 | tf_op jit(solution)/shard_map/potential/pallas_call | solution.py:573
  72.2 0.0 collective-permute-done.5.rest_0_
  72.2 0.0 collective-permute-done.6.rest_1_
  72.2 0.0 collective-permute-done.8.rest_3_
  72.2 0.0 collective-permute-done.9.rest_4_
  72.3 0.0 copy-start.27
  72.3 0.0 collective-permute-done.7.rest_2_
  72.3 0.5 copy-done.24
  72.8 0.0 copy-done.25
  72.8 0.0 copy-done.26
  72.9 0.0 copy-done.27
  72.9 0.0 copy-done.22
  72.9 2.2 %gather.1 = f32[128,512]{1,0:T(8,128)} custom-call(s32[1,2,2,16]{3,2,1,0:T(2,128)} %quad_ref.3, f32[128,512]{1,0:T(8,128)} %copy-done.2, f32[6,24,192]{2,1,0:T(8,128)} %potential.1._, bf16[32,512]{1,0:T(8,128)(2,1)} %copy-done.24, bf16[32,512]{1,0:T(8,128)(2,1)} %copy-done.25, bf16[64,512]{1,0:T(8,128)(2,1)} %copy-done.22, bf16[32,512]{1,0:T(8,128)(2,1)} %copy-done.26, ...), custom_call_target="tpu_custom_call" | custom-call | tf_op jit(solution)/shard_map/gather/pallas_call | solution.py:692
  (23 shorter events, 0.0 us)
Async XLA Ops:
  0.6 10.8 %copy-start.23 = (s32[8192]{0:T(1024)S(1)}, s32[8192]{0:T(1024)}, u32[]{:S(2)}) copy-start(s32[8192]{0:T(1024)} %param.25) | copy-start | bytes 98308
  2.4 9.2 %copy-start.21 = (f32[3,8192]{1,0:T(4,128)S(1)}, f32[3,8192]{1,0:T(4,128)}, u32[]{:S(2)}) copy-start(f32[3,8192]{1,0:T(4,128)} %param.27) | copy-start | bytes 294916
  2.4 12.2 %collective-permute-start.2 = (bf16[64,512]{1,0:T(8,128)(2,1)}, bf16[64,512]{1,0:T(8,128)(2,1)S(1)}, u32[]{:S(2)}, u32[]{:S(2)}) collective-permute-start(bf16[64,512]{1,0:T(8,128)(2,1)} %get-tuple-element.26), channel_id=1, source_target_pairs={{1,0},{0,1},{3,2},{2,3},{5,4},{4,5},{7,6},{6,7},{9,8},{8,9},{11,10... | collective-permute-start | bytes 196616 | tf_op jit(solution)/shard_map/ppermute | solution.py:47
  5.4 9.2 %collective-permute-start = (bf16[32,512]{1,0:T(8,128)(2,1)}, bf16[32,512]{1,0:T(8,128)(2,1)S(1)}, u32[]{:S(2)}, u32[]{:S(2)}) collective-permute-start(bf16[32,512]{1,0:T(8,128)(2,1)} %get-tuple-element.24), channel_id=1, source_target_pairs={{31,0},{30,1},{1,2},{0,3},{3,4},{2,5},{5,6},{4,7},{7,8},{6,9},{9,1... | collective-permute-start | bytes 98312 | tf_op jit(solution)/shard_map/ppermute | solution.py:47
  5.4 9.2 %collective-permute-start.1 = (bf16[32,512]{1,0:T(8,128)(2,1)}, bf16[32,512]{1,0:T(8,128)(2,1)S(1)}, u32[]{:S(2)}, u32[]{:S(2)}) collective-permute-start(bf16[32,512]{1,0:T(8,128)(2,1)} %get-tuple-element.25), channel_id=1, source_target_pairs={{30,0},{31,1},{0,2},{1,3},{2,4},{3,5},{4,6},{5,7},{6,8},{7,9},{8,1... | collective-permute-start | bytes 98312 | tf_op jit(solution)/shard_map/ppermute | solution.py:47
  7.0 7.7 %collective-permute-start.3 = (bf16[32,512]{1,0:T(8,128)(2,1)}, bf16[32,512]{1,0:T(8,128)(2,1)S(1)}, u32[]{:S(2)}, u32[]{:S(2)}) collective-permute-start(bf16[32,512]{1,0:T(8,128)(2,1)} %get-tuple-element.27), channel_id=1, source_target_pairs={{3,0},{2,1},{5,2},{4,3},{7,4},{6,5},{9,6},{8,7},{11,8},{10,9},{13,... | collective-permute-start | bytes 98312 | tf_op jit(solution)/shard_map/ppermute | solution.py:47
  10.8 3.9 %collective-permute-start.4 = (bf16[32,512]{1,0:T(8,128)(2,1)}, bf16[32,512]{1,0:T(8,128)(2,1)S(1)}, u32[]{:S(2)}, u32[]{:S(2)}) collective-permute-start(bf16[32,512]{1,0:T(8,128)(2,1)} %get-tuple-element.28), channel_id=1, source_target_pairs={{2,0},{3,1},{4,2},{5,3},{6,4},{7,5},{8,6},{9,7},{10,8},{11,9},{12,... | collective-permute-start | bytes 98312 | tf_op jit(solution)/shard_map/ppermute | solution.py:47
  11.6 0.9 %copy-start.4 = (bf16[64,896]{1,0:T(8,128)(2,1)S(1)}, bf16[64,896]{1,0:T(8,128)(2,1)}, u32[]{:S(2)}) copy-start(bf16[64,896]{1,0:T(8,128)(2,1)} %weight_radial_ref.1) | copy-start | bytes 344068
  11.6 0.9 %copy-start.8 = (f32[8,64]{1,0:T(8,128)S(1)}, f32[8,64]{1,0:T(8,128)}, u32[]{:S(2)}) copy-start(f32[8,64]{1,0:T(8,128)} %basis_weight_ref.1) | copy-start | bytes 6148
  11.6 0.9 %copy-start.11 = (s32[128]{0:T(128)S(1)}, s32[128]{0:T(128)}, u32[]{:S(2)}) copy-start(s32[128]{0:T(128)} %param.26) | copy-start | bytes 1540
  11.6 3.0 %copy-start.6 = (f32[128,128]{1,0:T(8,128)S(1)}, f32[128,128]{1,0:T(8,128)}, u32[]{:S(2)}) copy-start(f32[128,128]{1,0:T(8,128)} %weight_vector_ref.1) | copy-start | bytes 196612
  11.7 3.0 %copy-start.7 = (f32[128,128]{1,0:T(8,128)S(1)}, f32[128,128]{1,0:T(8,128)}, u32[]{:S(2)}) copy-start(f32[128,128]{1,0:T(8,128)} %weight_tensor_ref.1) | copy-start | bytes 196612
  11.8 0.9 %copy-start = (bf16[128,512]{1,0:T(8,128)(2,1)S(1)}, bf16[128,512]{1,0:T(8,128)(2,1)}, u32[]{:S(2)}) copy-start(bf16[128,512]{1,0:T(8,128)(2,1)} %features_ref.5) | copy-start | bytes 393220
  11.8 2.9 %copy-start.1 = (bf16[128,1152]{1,0:T(8,128)(2,1)S(1)}, bf16[128,1152]{1,0:T(8,128)(2,1)}, u32[]{:S(2)}) copy-start(bf16[128,1152]{1,0:T(8,128)(2,1)} %cotangent_ref.1) | copy-start | bytes 884740
  12.7 2.0 %copy-start.3 = (f32[128,256]{1,0:T(8,128)S(1)}, f32[128,256]{1,0:T(8,128)}, u32[]{:S(2)}) copy-start(f32[128,256]{1,0:T(8,128)} %weight_gate_ref.1) | copy-start | bytes 393220
  12.7 2.0 %copy-start.5 = (f32[128,128]{1,0:T(8,128)S(1)}, f32[128,128]{1,0:T(8,128)}, u32[]{:S(2)}) copy-start(f32[128,128]{1,0:T(8,128)} %weight_scalar_ref.1) | copy-start | bytes 196612
  14.6 0.7 copy-start.10
  14.7 0.7 copy-start.9
  14.7 0.7 copy-start.12
  15.4 38.9 %copy-start.14 = (bf16[384,192]{1,0:T(8,128)(2,1)S(1)}, bf16[384,192]{1,0:T(8,128)(2,1)}, u32[]{:S(2)}) copy-start(bf16[384,192]{1,0:T(8,128)(2,1)} %constant.16.clone.wave_z_ref) | copy-start | bytes 442372
  15.4 38.9 %copy-start.16 = (f32[96,1]{1,0:T(8,128)S(1)}, f32[96,1]{1,0:T(8,128)}, u32[]{:S(2)}) copy-start(f32[96,1]{1,0:T(8,128)} %constant.22.clone.square_x_ref) | copy-start | bytes 1156
  15.4 38.9 %copy-start.17 = (bf16[192,128]{1,0:T(8,128)(2,1)S(1)}, bf16[192,128]{1,0:T(8,128)(2,1)}, u32[]{:S(2)}) copy-start(bf16[192,128]{1,0:T(8,128)(2,1)} %constant.18.clone.wave_x_ref) | copy-start | bytes 147460
  15.4 38.9 %copy-start.18 = (f32[48,48]{1,0:T(8,128)S(1)}, f32[48,48]{1,0:T(8,128)}, u32[]{:S(2)}) copy-start(f32[48,48]{1,0:T(8,128)} %constant.20.clone.own_y_ref) | copy-start | bytes 27652
  15.4 38.9 %copy-start.19 = (bf16[96,48]{1,0:T(8,128)(2,1)S(1)}, bf16[96,48]{1,0:T(8,128)(2,1)}, u32[]{:S(2)}) copy-start(bf16[96,48]{1,0:T(8,128)(2,1)} %constant.17.clone.wave_y_ref) | copy-start | bytes 27652
  41.2 0.7 copy-start.2
  41.9 12.4 %copy-start.13 = (f32[192,192]{1,0:T(8,128)S(1)}, f32[192,192]{1,0:T(8,128)}, u32[]{:S(2)}) copy-start(f32[192,192]{1,0:T(8,128)} %constant.21.clone.own_z_ref) | copy-start | bytes 442372
  41.9 12.4 %copy-start.15 = (bf16[256,96]{1,0:T(8,128)(2,1)S(1)}, bf16[256,96]{1,0:T(8,128)(2,1)}, u32[]{:S(2)}) copy-start(bf16[256,96]{1,0:T(8,128)(2,1)} %constant.19.clone.own_x_ref) | copy-start | bytes 147460
  41.9 12.4 %all-to-all-start = ((f32[32,8,128]{2,1,0:T(8,128)}), f32[32,8,128]{2,1,0:T(8,128)S(1)}, u32[]{:S(2)}, u32[]{:S(2)}) async-start(f32[32,8,128]{2,1,0:T(8,128)} %get-tuple-element.31), calls=%async_computation | async-start | bytes 262144 | tf_op jit(solution)/shard_map/all_to_all | solution.py:593
  45.6 26.6 %collective-permute-start.5 = (bf16[32,512]{1,0:T(8,128)(2,1)S(1)}, bf16[32,512]{1,0:T(8,128)(2,1)S(1)}, u32[]{:S(2)}, u32[]{:S(2)}) collective-permute-start(bf16[32,512]{1,0:T(8,128)(2,1)S(1)} %get-tuple-element.32), channel_id=1, source_target_pairs={{3,0},{2,1},{5,2},{4,3},{7,4},{6,5},{9,6},{8,7},{11,8},{10,9},{13,... | collective-permute-start | bytes 98312 | tf_op jit(solution)/shard_map/ppermute | solution.py:47
  50.8 21.4 %collective-permute-start.6 = (bf16[32,512]{1,0:T(8,128)(2,1)S(1)}, bf16[32,512]{1,0:T(8,128)(2,1)S(1)}, u32[]{:S(2)}, u32[]{:S(2)}) collective-permute-start(bf16[32,512]{1,0:T(8,128)(2,1)S(1)} %get-tuple-element.33), channel_id=1, source_target_pairs={{2,0},{3,1},{4,2},{5,3},{6,4},{7,5},{8,6},{9,7},{10,8},{11,9},{12,... | collective-permute-start | bytes 98312 | tf_op jit(solution)/shard_map/ppermute | solution.py:47
  51.4 20.8 %collective-permute-start.8 = (bf16[32,512]{1,0:T(8,128)(2,1)S(1)}, bf16[32,512]{1,0:T(8,128)(2,1)S(1)}, u32[]{:S(2)}, u32[]{:S(2)}) collective-permute-start(bf16[32,512]{1,0:T(8,128)(2,1)S(1)} %get-tuple-element.35), channel_id=1, source_target_pairs={{31,0},{30,1},{1,2},{0,3},{3,4},{2,5},{5,6},{4,7},{7,8},{6,9},{9,1... | collective-permute-start | bytes 98312 | tf_op jit(solution)/shard_map/ppermute | solution.py:47
  51.5 20.8 %collective-permute-start.9 = (bf16[32,512]{1,0:T(8,128)(2,1)S(1)}, bf16[32,512]{1,0:T(8,128)(2,1)S(1)}, u32[]{:S(2)}, u32[]{:S(2)}) collective-permute-start(bf16[32,512]{1,0:T(8,128)(2,1)S(1)} %get-tuple-element.36), channel_id=1, source_target_pairs={{30,0},{31,1},{0,2},{1,3},{2,4},{3,5},{4,6},{5,7},{6,8},{7,9},{8,1... | collective-permute-start | bytes 98312 | tf_op jit(solution)/shard_map/ppermute | solution.py:47
  51.5 2.9 %copy-start.20 = (f32[1,192]{1,0:T(1,128)S(1)}, f32[1,192]{1,0:T(1,128)}, u32[]{:S(2)}) copy-start(f32[1,192]{1,0:T(1,128)} %constant.23.clone.square_z_ref) | copy-start | bytes 2308
  51.5 20.8 %collective-permute-start.7 = (bf16[64,512]{1,0:T(8,128)(2,1)S(1)}, bf16[64,512]{1,0:T(8,128)(2,1)S(1)}, u32[]{:S(2)}, u32[]{:S(2)}) collective-permute-start(bf16[64,512]{1,0:T(8,128)(2,1)S(1)} %get-tuple-element.34), channel_id=1, source_target_pairs={{1,0},{0,1},{3,2},{2,3},{5,4},{4,5},{7,6},{6,7},{9,8},{8,9},{11,10... | collective-permute-start | bytes 196616 | tf_op jit(solution)/shard_map/ppermute | solution.py:47
  72.2 0.6 copy-start.24
  72.2 0.6 copy-start.25
  72.2 0.6 copy-start.26
  72.3 0.6 copy-start.27
  72.3 0.6 copy-start.22

commit v2 on v1

--- a/solution.py
+++ b/solution.py
@@ -22,10 +22,12 @@
 BORDER = ((0, 0), (0, 1), (0, 2), (0, 3), (1, 0), (1, 3), (2, 0), (2, 3), (3, 0), (3, 1), (3, 2), (3, 3))
 SHIFT = (-1, 0, 0, 1)
 QUARTER = (1, 0, 1, 0)
-SLOT_BLOCK = 4
+SLOT_BLOCK = 8
 WORK = jnp.bfloat16
 ROW_GROUP = 16
 PIECE = 128
+LINES = 8
+SOLVE_UNROLL = 1
 VMEM_LIMIT = 48 * 1024 * 1024
 
 
@@ -444,13 +446,18 @@
     own_x[:, :cells_x] = (wave_x * damp_x[None, :]).reshape(bricks, cells_x, full_x)
     own_x = np.concatenate([split_np(block) for block in own_x], axis=0)
     scale = COUPLING / (full_x * full_y * cells_z)
+    extra = -cells_z % 128
+    tail = lambda value, fill, axis: np.pad(
+        value, [(0, extra) if dim == axis else (0, 0) for dim in range(value.ndim)], constant_values=fill
+    )
+    square_z = tail(square_z, 1.0, 0)
     return (
-        split_np(wave_z),
+        split_np(tail(wave_z, 0.0, 0)),
         split_np(wave_y),
         split_np(wave_x[:, window.reshape(-1)]),
         own_x,
         (wave_y * damp_y[None, :]).astype(np.float32),
-        (wave_z * damp_z[:, None] * scale).astype(np.float32),
+        tail(wave_z * damp_z[:, None] * scale, 0.0, 0).astype(np.float32),
         square_x.reshape(-1, 1).astype(np.float32),
         square_z.reshape(1, -1).astype(np.float32),
     )
@@ -504,7 +511,8 @@
     cells_x, _, cells_z = out_ref.shape
     window = cells_x + 2
     full_y = planes_ref.shape[0]
-    chunk = lines_ref.shape[0]
+    lanes_z = square_ref.shape[1]
+    chunk = lines_ref.shape[1] // lanes_z
 
     @pl.when(step == 0)
     def _():
@@ -536,31 +544,39 @@
         z_high, z_low = shape_z_ref[brick, 0], shape_z_ref[brick, 1]
         across = ((1,), (1,))
         grid = dot_t(high, z_high, across) + dot_t(high, z_low, across) + dot_t(low, z_high, across)
-        lines_ref[:, pl.ds(pl.multiple_of(brick * window, window), window), :] = grid.reshape(
-            chunk, window, cells_z
-        )
+        place = pl.ds(pl.multiple_of(brick * window, window), window)
+        for line in range(chunk):
+            lines_ref[place, line * lanes_z : (line + 1) * lanes_z] = grid[line * window : (line + 1) * window]
         return carry
 
     lax.fori_loop(0, bricks, spread, 0, unroll=2)
     own = pl.multiple_of(lax.axis_index("brick") * (2 * window), 2 * window)
 
-    def solve(line, carry):
-        wave = dot_split(wave_x_ref[...], split_f32(lines_ref[line]))
-        number = first + line
-        height = jnp.minimum(number, full_y - number).astype(jnp.float32) * (1.0 / full_y)
-        square = square_ref[...] + height * height
-        wave = wave * jnp.where(square > 0.0, 1.0 / jnp.where(square > 0.0, square, 1.0), 0.0)
-        planes_ref[number] = dot_split(own_x_ref[pl.ds(own, 2 * window), :], split_f32(wave))
+    def solve(batch, carry):
+        lanes = pl.ds(pl.multiple_of(batch * (LINES * lanes_z), LINES * lanes_z), LINES * lanes_z)
+        wave = dot_split(wave_x_ref[...], split_f32(lines_ref[:, lanes]))
+        squares = []
+        for line in range(LINES):
+            number = first + batch * LINES + line
+            height = jnp.minimum(number, full_y - number).astype(jnp.float32) * (1.0 / full_y)
+            squares.append(square_ref[...] + height * height)
+        square = jnp.concatenate(squares, axis=1)
+        inverse = pl.reciprocal(square, approx=True)
+        inverse = inverse * (2.0 - square * inverse)
+        wave = wave * jnp.where(square > 0.0, inverse, 0.0)
+        planes = dot_split(own_x_ref[pl.ds(own, 2 * window), :], split_f32(wave))
+        for line in range(LINES):
+            planes_ref[first + batch * LINES + line] = planes[:, line * lanes_z : (line + 1) * lanes_z]
         return carry
 
-    lax.fori_loop(0, chunk, solve, 0, unroll=8)
+    lax.fori_loop(0, chunk // LINES, solve, 0, unroll=SOLVE_UNROLL)
 
     @pl.when(step == pl.num_programs(0) - 1)
     def _():
         along_y = own_y_ref[pl.ds(pl.multiple_of(lax.axis_index("pme") * cells_y, 8), cells_y), :]
-        for plane in range(cells_x):
-            lines = dot_f32(along_y, planes_ref[:, plane, :])
-            out_ref[plane] = dot_f32(lines, own_z_ref[...])
+        lines = [dot_f32(along_y, planes_ref[:, plane, :]) for plane in range(cells_x)]
+        block = dot_f32(jnp.concatenate(lines, axis=0), own_z_ref[...])
+        out_ref[...] = block.reshape(cells_x, cells_y, cells_z)
 
 
 def potential_block(gathered, cells_x, cells_y, cells_z):
@@ -570,6 +586,7 @@
     window = cells_x + 2
     tables = grid_tables(bricks, cells_x, cells_y, full_y, cells_z)
     chunk = full_y if full_y <= 48 else 16
+    lanes_z = cells_z + -cells_z % 128
     return pl.pallas_call(
         functools.partial(potential_kernel, cells_y),
         grid=(full_y // chunk,),
@@ -577,10 +594,10 @@
         out_specs=whole((cells_x, cells_y, cells_z)),
         out_shape=jax.ShapeDtypeStruct((cells_x, cells_y, cells_z), jnp.float32),
         scratch_shapes=[
-            pltpu.VMEM((bricks, 2, cells_z, atoms), jnp.bfloat16),
-            pltpu.VMEM((chunk, bricks * window, cells_z), jnp.float32),
-            pltpu.VMEM((bricks * cells_x, cells_z), jnp.float32),
-            pltpu.VMEM((full_y, window, cells_z), jnp.float32),
+            pltpu.VMEM((bricks, 2, lanes_z, atoms), jnp.bfloat16),
+            pltpu.VMEM((bricks * window, chunk * lanes_z), jnp.float32),
+            pltpu.VMEM((bricks * cells_x, lanes_z), jnp.float32),
+            pltpu.VMEM((full_y, window, lanes_z), jnp.float32),
         ],
         compiler_params=params(),
         cost_estimate=pl.CostEstimate(flops=2 * 10**10, bytes_accessed=10**7, transcendentals=0),

time: 75.4 us -> 70.7 us (0.938)
  Pallas kernels: 49.6 us -> 44.9 us
    pallas_call x1, Pallas kernels: 17.8 us -> 13.6 us  [potential_block(): pl.pallas_call(functools.partial(potential_kernel, cells_y), grid=(full_y...]
  transfers between devices with their start and end apart: 11 -> 11, of which waited for: 1 -> 1; matrix products, arithmetic and copies ran while one was open for 1% -> 1% of each run, Pallas kernels for 26% -> 22%
where the time goes in v2:
time: 70.7 us; the launch traced here: 70.4 us
  Pallas kernels  44.9 us (64%)
  starting transfers between devices  20 us (28%)
  local copies, waits for them, and re-layouts  3.24 us (5%)
  waiting for transfers between devices  1.33 us (2%)
  between operations  0.96 us (1%)
    pallas_call x1, Pallas kernels, per_device(): pl.pallas_call(functools.partial(layer_kernel, groups), out_shape=[jax.Sh...  25.4 us
    ppermute x10, starting transfers between devices, shifted(): return lax.ppermute(value, ('brick', 'pme'), pairs)  16.4 us
    pallas_call x1, Pallas kernels, potential_block(): pl.pallas_call(functools.partial(potential_kernel, cells_y), grid=(full_y...  13.6 us
    all_to_all x1, starting transfers between devices, all_charges(): lax.all_to_all(copies, ('brick', 'pme'), split_axis=0, concat_axis=0, til...  3.62 us
    unnamed x56, local copies, waits for them, and re-layouts  2.83 us
    pallas_call x1, Pallas kernels, per_device(): pl.pallas_call(functools.partial(gather_kernel, groups), in_specs=[pl.Blo...  2.22 us
    pallas_call x1, Pallas kernels, per_device(): pl.pallas_call(radial_kernel, out_shape=[jax.ShapeDtypeStruct((hidden_uni...  1.86 us
    pallas_call x1, Pallas kernels, per_device(): pl.pallas_call(functools.partial(pack_kernel, groups), out_shape=message_...  1.8 us
  transfers between devices with their start and end apart: 11, of which 1 were waited for; matrix products, arithmetic and copies ran while one was open for 1% of the time, Pallas kernels for 22%

profile of v2, /device:TPU:0, one launch (start us, length us, event | category | flops | bytes accessed | tf_op | source)
XLA Modules:
  0.0 70.4 jit_solution(12444484686191544311)
XLA Ops:
  0.6 0.0 copy-start.23
  0.6 1.8 %pack.1 = (bf16[32,512]{1,0:T(8,128)(2,1)}, bf16[32,512]{1,0:T(8,128)(2,1)}, bf16[64,512]{1,0:T(8,128)(2,1)}, bf16[32,512]{1,0:T(8,128)(2,1)}, bf16[32,512]{1,0:T(8,128)(2,1)}) custom-call(s32[1,2,2,16]{3,2,1,0:T(2,128)} %quad_ref.3, bf16[128,512]{1,0:T(8,128)(2,1)} %features_ref.5), custom_call_target="tpu_custom_call" | custom-call | tf_op jit(solution)/shard_map/pack/pallas_call | solution.py:642
  2.4 3.0 %collective-permute-start.2 = (bf16[64,512]{1,0:T(8,128)(2,1)}, bf16[64,512]{1,0:T(8,128)(2,1)S(1)}, u32[]{:S(2)}, u32[]{:S(2)}) collective-permute-start(bf16[64,512]{1,0:T(8,128)(2,1)} %get-tuple-element.26), channel_id=1, source_target_pairs={{1,0},{0,1},{3,2},{2,3},{5,4},{4,5},{7,6},{6,7},{9,8},{8,9},{11,10... | collective-permute-start | bytes 196616 | tf_op jit(solution)/shard_map/ppermute | solution.py:49
  5.4 0.0 collective-permute-start
  5.4 1.5 %collective-permute-start.1 = (bf16[32,512]{1,0:T(8,128)(2,1)}, bf16[32,512]{1,0:T(8,128)(2,1)S(1)}, u32[]{:S(2)}, u32[]{:S(2)}) collective-permute-start(bf16[32,512]{1,0:T(8,128)(2,1)} %get-tuple-element.25), channel_id=1, source_target_pairs={{30,0},{31,1},{0,2},{1,3},{2,4},{3,5},{4,6},{5,7},{6,8},{7,9},{8,1... | collective-permute-start | bytes 98312 | tf_op jit(solution)/shard_map/ppermute | solution.py:49
  7.0 3.8 %collective-permute-start.3 = (bf16[32,512]{1,0:T(8,128)(2,1)}, bf16[32,512]{1,0:T(8,128)(2,1)S(1)}, u32[]{:S(2)}, u32[]{:S(2)}) collective-permute-start(bf16[32,512]{1,0:T(8,128)(2,1)} %get-tuple-element.27), channel_id=1, source_target_pairs={{3,0},{2,1},{5,2},{4,3},{7,4},{6,5},{9,6},{8,7},{11,8},{10,9},{13,... | collective-permute-start | bytes 98312 | tf_op jit(solution)/shard_map/ppermute | solution.py:49
  10.8 0.7 collective-permute-start.4
  11.4 0.0 copy-done.23
  11.4 0.1 reshape.23
  11.5 0.1 copy.27
  11.6 0.0 copy-done.21
  11.6 0.0 copy-start.4
  11.6 0.0 copy-start.8
  11.6 0.0 copy-start.11
  11.6 0.0 copy-start.6
  11.7 0.0 copy-start.7
  11.7 0.2 reshape.21
  11.8 0.1 copy.26
  11.9 0.6 copy-done.4
  12.5 0.0 copy-done.8
  12.5 0.2 copy-done
  12.7 1.9 %radial.1 = (bf16[64,8192]{1,0:T(8,128)(2,1)S(1)}, f32[3,64,128]{2,1,0:T(8,128)S(1)}, bf16[896,64]{1,0:T(8,128)(2,1)S(1)}, bf16[512,128]{1,0:T(8,128)(2,1)S(1)}) custom-call(f32[3,64,128]{2,1,0:T(8,128)S(1)} %bitcast.5, s32[1,128]{1,0:T(1,128)S(1)} %bitcast.8, f32[8,64]{1,0:T(8,128)S(1)} %copy-done.8, bf16[64,896]{1,0:T(8,128)(2,1)S(1)} %copy-done.4, ...), custom_call_target="tpu_custom_call" | custom-call | tf_op jit(solution)/shard_map/radial/pallas_call | solution.py:649
  14.6 0.0 collective-permute-done.rest_0_
  14.6 0.0 collective-permute-done.1.rest_1_
  14.6 0.0 collective-permute-done.3.rest_3_
  14.6 0.0 collective-permute-done.4.rest_4_
  14.6 0.0 collective-permute-done.2.rest_2_
  14.7 0.0 copy-start.10
  14.7 0.0 copy-start.9
  14.7 0.0 copy-start.12
  14.7 0.0 copy-done.6
  14.7 0.0 copy-done.7
  14.7 0.0 copy-done.1
  14.7 0.0 copy-done.3
  14.7 0.0 copy-done.5
  14.7 0.6 copy-done.10
  15.3 0.0 copy-done.9
  15.4 0.0 copy-done.12
  15.4 0.0 copy-start.17
  15.4 0.0 copy-start.18
  15.4 0.0 copy-start.19
  15.4 25.4 %layer.1 = (bf16[128,1152]{1,0:T(8,128)(2,1)}, f32[32,8,128]{2,1,0:T(8,128)}, f32[128,512]{1,0:T(8,128)S(1)}, bf16[32,512]{1,0:T(8,128)(2,1)S(1)}, bf16[32,512]{...) custom-call(bf16[64,8192]{1,0:T(8,128)(2,1)S(1)} %get-tuple-element.20., ...), custom_call_target="tpu_custom_call" | custom-call | tf_op jit(solution)/shard_map/layer/pallas_call | solution.py:665
  40.8 0.7 copy-done.2
  41.5 3.6 %all-to-all-start = ((f32[32,8,128]{2,1,0:T(8,128)}), f32[32,8,128]{2,1,0:T(8,128)S(1)}, u32[]{:S(2)}, u32[]{:S(2)}) async-start(f32[32,8,128]{2,1,0:T(8,128)} %get-tuple-element.31), calls=%async_computation | async-start | bytes 262144 | tf_op jit(solution)/shard_map/all_to_all | solution.py:610
  45.2 5.3 %collective-permute-start.5 = (bf16[32,512]{1,0:T(8,128)(2,1)S(1)}, bf16[32,512]{1,0:T(8,128)(2,1)S(1)}, u32[]{:S(2)}, u32[]{:S(2)}) collective-permute-start(bf16[32,512]{1,0:T(8,128)(2,1)S(1)} %get-tuple-element.32), channel_id=1, source_target_pairs={{3,0},{2,1},{5,2},{4,3},{7,4},{6,5},{9,6},{8,7},{11,8},{10,9},{13,... | collective-permute-start | bytes 98312 | tf_op jit(solution)/shard_map/ppermute | solution.py:49
  50.4 0.5 collective-permute-start.6
  51.0 0.1 collective-permute-start.8
  51.1 0.0 collective-permute-start.9
  51.1 1.5 %collective-permute-start.7 = (bf16[64,512]{1,0:T(8,128)(2,1)S(1)}, bf16[64,512]{1,0:T(8,128)(2,1)S(1)}, u32[]{:S(2)}, u32[]{:S(2)}) collective-permute-start(bf16[64,512]{1,0:T(8,128)(2,1)S(1)} %get-tuple-element.34), channel_id=1, source_target_pairs={{1,0},{0,1},{3,2},{2,3},{5,4},{4,5},{7,6},{6,7},{9,8},{8,9},{11,10... | collective-permute-start | bytes 196616 | tf_op jit(solution)/shard_map/ppermute | solution.py:49
  52.6 1.3 %all-to-all-done = f32[32,8,128]{2,1,0:T(8,128)S(1)} async-done(((f32[32,8,128]{2,1,0:T(8,128)}), f32[32,8,128]{2,1,0:T(8,128)S(1)}, u32[]{:S(2)}, u32[]{:S(2)}) %all-to-all-start) | async-done | bytes 131104 | tf_op jit(solution)/shard_map/all_to_all | solution.py:610
  53.9 0.0 copy-done.15
  53.9 13.6 %potential.1._ = f32[6,24,192]{2,1,0:T(8,128)} custom-call(f32[16,2,8,128]{3,2,1,0:T(8,128)S(1)} %bitcast.7, bf16[512,192]{1,0:T(8,128)(2,1)S(1)} %copy-done.14, bf16[96,48]{1,0:T(8,128)(2,1)S(1)} %copy-done.19, bf16[192,128]{1,0:T(8,128)(2,1)S(1)} %copy-done.17, bf16[256,96]{1,0:T(8,128)(2,1)S(1)} %copy-done.15, f32[48,48]{1,0:T(8,128)S(1)} %copy-done.18, ...), custom_call_target="tpu_custom_call" | custom-call | flops 20000000000 | bytes 10000000 | tf_op jit(solution)/shard_map/potential/pallas_call | solution.py:590
  67.5 0.0 collective-permute-done.5.rest_0_
  67.5 0.0 collective-permute-done.6.rest_1_
  67.5 0.0 collective-permute-done.8.rest_3_
  67.5 0.0 collective-permute-done.9.rest_4_
  67.6 0.0 copy-start.27
  67.6 0.0 collective-permute-done.7.rest_2_
  67.6 0.5 copy-done.24
  68.1 0.0 copy-done.25
  68.1 0.0 copy-done.26
  68.2 0.0 copy-done.27
  68.2 0.0 copy-done.22
  68.2 2.2 %gather.1 = f32[128,512]{1,0:T(8,128)} custom-call(s32[1,2,2,16]{3,2,1,0:T(2,128)} %quad_ref.3, f32[128,512]{1,0:T(8,128)} %copy-done.2, f32[6,24,192]{2,1,0:T(8,128)} %potential.1._, bf16[32,512]{1,0:T(8,128)(2,1)} %copy-done.24, bf16[32,512]{1,0:T(8,128)(2,1)} %copy-done.25, bf16[64,512]{1,0:T(8,128)(2,1)} %copy-done.22, bf16[32,512]{1,0:T(8,128)(2,1)} %copy-done.26, ...), custom_call_target="tpu_custom_call" | custom-call | tf_op jit(solution)/shard_map/gather/pallas_call | solution.py:709
  (23 shorter events, 0.0 us)
Async XLA Ops:
  0.6 10.8 %copy-start.23 = (s32[8192]{0:T(1024)S(1)}, s32[8192]{0:T(1024)}, u32[]{:S(2)}) copy-start(s32[8192]{0:T(1024)} %param.25) | copy-start | bytes 98308
  2.4 9.2 %copy-start.21 = (f32[3,8192]{1,0:T(4,128)S(1)}, f32[3,8192]{1,0:T(4,128)}, u32[]{:S(2)}) copy-start(f32[3,8192]{1,0:T(4,128)} %param.27) | copy-start | bytes 294916
  2.4 12.2 %collective-permute-start.2 = (bf16[64,512]{1,0:T(8,128)(2,1)}, bf16[64,512]{1,0:T(8,128)(2,1)S(1)}, u32[]{:S(2)}, u32[]{:S(2)}) collective-permute-start(bf16[64,512]{1,0:T(8,128)(2,1)} %get-tuple-element.26), channel_id=1, source_target_pairs={{1,0},{0,1},{3,2},{2,3},{5,4},{4,5},{7,6},{6,7},{9,8},{8,9},{11,10... | collective-permute-start | bytes 196616 | tf_op jit(solution)/shard_map/ppermute | solution.py:49
  5.4 9.2 %collective-permute-start = (bf16[32,512]{1,0:T(8,128)(2,1)}, bf16[32,512]{1,0:T(8,128)(2,1)S(1)}, u32[]{:S(2)}, u32[]{:S(2)}) collective-permute-start(bf16[32,512]{1,0:T(8,128)(2,1)} %get-tuple-element.24), channel_id=1, source_target_pairs={{31,0},{30,1},{1,2},{0,3},{3,4},{2,5},{5,6},{4,7},{7,8},{6,9},{9,1... | collective-permute-start | bytes 98312 | tf_op jit(solution)/shard_map/ppermute | solution.py:49
  5.4 9.2 %collective-permute-start.1 = (bf16[32,512]{1,0:T(8,128)(2,1)}, bf16[32,512]{1,0:T(8,128)(2,1)S(1)}, u32[]{:S(2)}, u32[]{:S(2)}) collective-permute-start(bf16[32,512]{1,0:T(8,128)(2,1)} %get-tuple-element.25), channel_id=1, source_target_pairs={{30,0},{31,1},{0,2},{1,3},{2,4},{3,5},{4,6},{5,7},{6,8},{7,9},{8,1... | collective-permute-start | bytes 98312 | tf_op jit(solution)/shard_map/ppermute | solution.py:49
  7.0 7.7 %collective-permute-start.3 = (bf16[32,512]{1,0:T(8,128)(2,1)}, bf16[32,512]{1,0:T(8,128)(2,1)S(1)}, u32[]{:S(2)}, u32[]{:S(2)}) collective-permute-start(bf16[32,512]{1,0:T(8,128)(2,1)} %get-tuple-element.27), channel_id=1, source_target_pairs={{3,0},{2,1},{5,2},{4,3},{7,4},{6,5},{9,6},{8,7},{11,8},{10,9},{13,... | collective-permute-start | bytes 98312 | tf_op jit(solution)/shard_map/ppermute | solution.py:49
  10.8 3.9 %collective-permute-start.4 = (bf16[32,512]{1,0:T(8,128)(2,1)}, bf16[32,512]{1,0:T(8,128)(2,1)S(1)}, u32[]{:S(2)}, u32[]{:S(2)}) collective-permute-start(bf16[32,512]{1,0:T(8,128)(2,1)} %get-tuple-element.28), channel_id=1, source_target_pairs={{2,0},{3,1},{4,2},{5,3},{6,4},{7,5},{8,6},{9,7},{10,8},{11,9},{12,... | collective-permute-start | bytes 98312 | tf_op jit(solution)/shard_map/ppermute | solution.py:49
  11.6 0.9 %copy-start.4 = (bf16[64,896]{1,0:T(8,128)(2,1)S(1)}, bf16[64,896]{1,0:T(8,128)(2,1)}, u32[]{:S(2)}) copy-start(bf16[64,896]{1,0:T(8,128)(2,1)} %weight_radial_ref.1) | copy-start | bytes 344068
  11.6 0.9 %copy-start.8 = (f32[8,64]{1,0:T(8,128)S(1)}, f32[8,64]{1,0:T(8,128)}, u32[]{:S(2)}) copy-start(f32[8,64]{1,0:T(8,128)} %basis_weight_ref.1) | copy-start | bytes 6148
  11.6 0.9 %copy-start.11 = (s32[128]{0:T(128)S(1)}, s32[128]{0:T(128)}, u32[]{:S(2)}) copy-start(s32[128]{0:T(128)} %param.26) | copy-start | bytes 1540
  11.6 3.1 %copy-start.6 = (f32[128,128]{1,0:T(8,128)S(1)}, f32[128,128]{1,0:T(8,128)}, u32[]{:S(2)}) copy-start(f32[128,128]{1,0:T(8,128)} %weight_vector_ref.1) | copy-start | bytes 196612
  11.7 3.1 %copy-start.7 = (f32[128,128]{1,0:T(8,128)S(1)}, f32[128,128]{1,0:T(8,128)}, u32[]{:S(2)}) copy-start(f32[128,128]{1,0:T(8,128)} %weight_tensor_ref.1) | copy-start | bytes 196612
  11.8 0.9 %copy-start = (bf16[128,512]{1,0:T(8,128)(2,1)S(1)}, bf16[128,512]{1,0:T(8,128)(2,1)}, u32[]{:S(2)}) copy-start(bf16[128,512]{1,0:T(8,128)(2,1)} %features_ref.5) | copy-start | bytes 393220
  11.8 2.9 %copy-start.1 = (bf16[128,1152]{1,0:T(8,128)(2,1)S(1)}, bf16[128,1152]{1,0:T(8,128)(2,1)}, u32[]{:S(2)}) copy-start(bf16[128,1152]{1,0:T(8,128)(2,1)} %cotangent_ref.1) | copy-start | bytes 884740
  12.7 2.0 %copy-start.3 = (f32[128,256]{1,0:T(8,128)S(1)}, f32[128,256]{1,0:T(8,128)}, u32[]{:S(2)}) copy-start(f32[128,256]{1,0:T(8,128)} %weight_gate_ref.1) | copy-start | bytes 393220
  12.7 2.0 %copy-start.5 = (f32[128,128]{1,0:T(8,128)S(1)}, f32[128,128]{1,0:T(8,128)}, u32[]{:S(2)}) copy-start(f32[128,128]{1,0:T(8,128)} %weight_scalar_ref.1) | copy-start | bytes 196612
  14.7 0.7 copy-start.10
  14.7 0.7 copy-start.9
  14.7 0.7 copy-start.12
  15.4 38.5 %copy-start.14 = (bf16[512,192]{1,0:T(8,128)(2,1)S(1)}, bf16[512,192]{1,0:T(8,128)(2,1)}, u32[]{:S(2)}) copy-start(bf16[512,192]{1,0:T(8,128)(2,1)} %constant.16.clone.wave_z_ref) | copy-start | bytes 589828
  15.4 38.5 %copy-start.15 = (bf16[256,96]{1,0:T(8,128)(2,1)S(1)}, bf16[256,96]{1,0:T(8,128)(2,1)}, u32[]{:S(2)}) copy-start(bf16[256,96]{1,0:T(8,128)(2,1)} %constant.19.clone.own_x_ref) | copy-start | bytes 147460
  15.4 38.5 %copy-start.16 = (f32[96,1]{1,0:T(8,128)S(1)}, f32[96,1]{1,0:T(8,128)}, u32[]{:S(2)}) copy-start(f32[96,1]{1,0:T(8,128)} %constant.22.clone.square_x_ref) | copy-start | bytes 1156
  15.4 38.5 %copy-start.17 = (bf16[192,128]{1,0:T(8,128)(2,1)S(1)}, bf16[192,128]{1,0:T(8,128)(2,1)}, u32[]{:S(2)}) copy-start(bf16[192,128]{1,0:T(8,128)(2,1)} %constant.18.clone.wave_x_ref) | copy-start | bytes 147460
  15.4 38.5 %copy-start.18 = (f32[48,48]{1,0:T(8,128)S(1)}, f32[48,48]{1,0:T(8,128)}, u32[]{:S(2)}) copy-start(f32[48,48]{1,0:T(8,128)} %constant.20.clone.own_y_ref) | copy-start | bytes 27652
  15.4 38.5 %copy-start.19 = (bf16[96,48]{1,0:T(8,128)(2,1)S(1)}, bf16[96,48]{1,0:T(8,128)(2,1)}, u32[]{:S(2)}) copy-start(bf16[96,48]{1,0:T(8,128)(2,1)} %constant.17.clone.wave_y_ref) | copy-start | bytes 27652
  40.8 0.7 copy-start.2
  41.5 12.4 %copy-start.13 = (f32[256,192]{1,0:T(8,128)S(1)}, f32[256,192]{1,0:T(8,128)}, u32[]{:S(2)}) copy-start(f32[256,192]{1,0:T(8,128)} %constant.21.clone.own_z_ref) | copy-start | bytes 589828
  41.5 12.4 %all-to-all-start = ((f32[32,8,128]{2,1,0:T(8,128)}), f32[32,8,128]{2,1,0:T(8,128)S(1)}, u32[]{:S(2)}, u32[]{:S(2)}) async-start(f32[32,8,128]{2,1,0:T(8,128)} %get-tuple-element.31), calls=%async_computation | async-start | bytes 262144 | tf_op jit(solution)/shard_map/all_to_all | solution.py:610
  45.2 22.3 %collective-permute-start.5 = (bf16[32,512]{1,0:T(8,128)(2,1)S(1)}, bf16[32,512]{1,0:T(8,128)(2,1)S(1)}, u32[]{:S(2)}, u32[]{:S(2)}) collective-permute-start(bf16[32,512]{1,0:T(8,128)(2,1)S(1)} %get-tuple-element.32), channel_id=1, source_target_pairs={{3,0},{2,1},{5,2},{4,3},{7,4},{6,5},{9,6},{8,7},{11,8},{10,9},{13,... | collective-permute-start | bytes 98312 | tf_op jit(solution)/shard_map/ppermute | solution.py:49
  50.4 17.1 %collective-permute-start.6 = (bf16[32,512]{1,0:T(8,128)(2,1)S(1)}, bf16[32,512]{1,0:T(8,128)(2,1)S(1)}, u32[]{:S(2)}, u32[]{:S(2)}) collective-permute-start(bf16[32,512]{1,0:T(8,128)(2,1)S(1)} %get-tuple-element.33), channel_id=1, source_target_pairs={{2,0},{3,1},{4,2},{5,3},{6,4},{7,5},{8,6},{9,7},{10,8},{11,9},{12,... | collective-permute-start | bytes 98312 | tf_op jit(solution)/shard_map/ppermute | solution.py:49
  51.0 16.6 %collective-permute-start.8 = (bf16[32,512]{1,0:T(8,128)(2,1)S(1)}, bf16[32,512]{1,0:T(8,128)(2,1)S(1)}, u32[]{:S(2)}, u32[]{:S(2)}) collective-permute-start(bf16[32,512]{1,0:T(8,128)(2,1)S(1)} %get-tuple-element.35), channel_id=1, source_target_pairs={{31,0},{30,1},{1,2},{0,3},{3,4},{2,5},{5,6},{4,7},{7,8},{6,9},{9,1... | collective-permute-start | bytes 98312 | tf_op jit(solution)/shard_map/ppermute | solution.py:49
  51.1 16.5 %collective-permute-start.9 = (bf16[32,512]{1,0:T(8,128)(2,1)S(1)}, bf16[32,512]{1,0:T(8,128)(2,1)S(1)}, u32[]{:S(2)}, u32[]{:S(2)}) collective-permute-start(bf16[32,512]{1,0:T(8,128)(2,1)S(1)} %get-tuple-element.36), channel_id=1, source_target_pairs={{30,0},{31,1},{0,2},{1,3},{2,4},{3,5},{4,6},{5,7},{6,8},{7,9},{8,1... | collective-permute-start | bytes 98312 | tf_op jit(solution)/shard_map/ppermute | solution.py:49
  51.1 2.9 %copy-start.20 = (f32[1,256]{1,0:T(1,128)S(1)}, f32[1,256]{1,0:T(1,128)}, u32[]{:S(2)}) copy-start(f32[1,256]{1,0:T(1,128)} %constant.23.clone.square_z_ref) | copy-start | bytes 3076
  51.1 16.5 %collective-permute-start.7 = (bf16[64,512]{1,0:T(8,128)(2,1)S(1)}, bf16[64,512]{1,0:T(8,128)(2,1)S(1)}, u32[]{:S(2)}, u32[]{:S(2)}) collective-permute-start(bf16[64,512]{1,0:T(8,128)(2,1)S(1)} %get-tuple-element.34), channel_id=1, source_target_pairs={{1,0},{0,1},{3,2},{2,3},{5,4},{4,5},{7,6},{6,7},{9,8},{8,9},{11,10... | collective-permute-start | bytes 196616 | tf_op jit(solution)/shard_map/ppermute | solution.py:49
  67.5 0.6 copy-start.24
  67.5 0.6 copy-start.25
  67.5 0.6 copy-start.26
  67.6 0.6 copy-start.27
  67.6 0.6 copy-start.22

commit v3 on v2

--- a/solution.py
+++ b/solution.py
@@ -26,7 +26,7 @@
 WORK = jnp.bfloat16
 ROW_GROUP = 16
 PIECE = 128
-LINES = 8
+LINES = 16
 SOLVE_UNROLL = 1
 VMEM_LIMIT = 48 * 1024 * 1024
 
@@ -59,23 +59,33 @@
     return dot_t(left, right, dims, PRECISE)
 
 
+def dot_node(left, right, dims=((1,), (0,))):
+    left_high, left_low = split_f32(left)
+    right_high, right_low = split_f32(right)
+    return (
+        dot_t(left_high, right_high, dims) + dot_t(left_high, right_low, dims) + dot_t(left_low, right_high, dims)
+    )
+
+
 def params(**kwargs):
     return pltpu.CompilerParams(vmem_limit_bytes=VMEM_LIMIT, **kwargs)
 
 
+def quarter_onehot(quad_ref, atoms, quarters):
+    index = jnp.concatenate([quad_ref[0, row, col : col + 1, :] for row, col in quarters], axis=1)
+    rows = lax.broadcasted_iota(jnp.int32, (atoms, index.shape[1]), 0)
+    return (rows == index).astype(jnp.bfloat16)
+
+
 def pack_kernel(groups, quad_ref, features_ref, *message_refs):
-    atoms = features_ref.shape[0]
     ghost = quad_ref.shape[3]
-    rows = lax.broadcasted_iota(jnp.int32, (atoms, ghost), 0)
-    picked = {}
-    for row in range(2):
-        for col in range(2):
-            chosen = (rows == quad_ref[0, row, col : col + 1, :]).astype(jnp.bfloat16)
-            picked[row, col] = dot_t(chosen, features_ref[...], ((0,), (0,))).astype(jnp.bfloat16)
+    chosen = quarter_onehot(quad_ref, features_ref.shape[0], ((0, 0), (0, 1), (1, 0), (1, 1)))
+    picked = dot_t(chosen, features_ref[...], ((0,), (0,))).astype(jnp.bfloat16)
     for (_, cells), message_ref in zip(groups, message_refs):
         for place, cell in enumerate(cells):
             row, col = BORDER[cell]
-            message_ref[place * ghost : (place + 1) * ghost, :] = picked[QUARTER[row], QUARTER[col]]
+            lower = (2 * QUARTER[row] + QUARTER[col]) * ghost
+            message_ref[place * ghost : (place + 1) * ghost, :] = picked[lower : lower + ghost]
 
 
 def radial_kernel(
@@ -288,11 +298,11 @@
     sums += [0.5 * total_ref[7], 0.5 * total_ref[8], 0.5 * total_ref[9]]
     aggregate = [(block * scale).T for block in sums]
     columns = lambda ref, block: ref[:, block * channels : (block + 1) * channels].astype(jnp.float32)
-    gate = jax.nn.sigmoid(dot_f32(aggregate[0], weight_gate_ref[...]))
-    inner = dot_f32(aggregate[0], weight_scalar_ref[...])
+    gate = jax.nn.sigmoid(dot_node(aggregate[0], weight_gate_ref[...]))
+    inner = dot_node(aggregate[0], weight_scalar_ref[...])
     inner_sigmoid = jax.nn.sigmoid(inner)
-    vectors = dot_f32(jnp.concatenate(aggregate[1:4], axis=0), weight_vector_ref[...])
-    tensors = dot_f32(jnp.concatenate(aggregate[4:9], axis=0), weight_tensor_ref[...])
+    vectors = dot_node(jnp.concatenate(aggregate[1:4], axis=0), weight_vector_ref[...])
+    tensors = dot_node(jnp.concatenate(aggregate[4:9], axis=0), weight_tensor_ref[...])
     gate_v, gate_t = gate[:, :channels], gate[:, channels:]
     scalar_out = (columns(features_ref, 0) + inner * inner_sigmoid).astype(jnp.bfloat16)
     updated_ref[:, :channels] = scalar_out
@@ -326,10 +336,10 @@
     )
     gate_grad = jnp.concatenate([gate_grad_v, gate_grad_t], axis=1) * (gate * (1.0 - gate))
     across = ((1,), (1,))
-    grad_s = dot_f32(inner_grad, weight_scalar_ref[...], across)
-    grad_s = grad_s + dot_f32(gate_grad, weight_gate_ref[...], across)
-    grad_v = dot_f32(jnp.concatenate(grad_v, axis=0), weight_vector_ref[...], across)
-    grad_t = dot_f32(jnp.concatenate(grad_t, axis=0), weight_tensor_ref[...], across)
+    grad_s = dot_node(inner_grad, weight_scalar_ref[...], across)
+    grad_s = grad_s + dot_node(gate_grad, weight_gate_ref[...], across)
+    grad_v = dot_node(jnp.concatenate(grad_v, axis=0), weight_vector_ref[...], across)
+    grad_t = dot_node(jnp.concatenate(grad_t, axis=0), weight_tensor_ref[...], across)
     t00, t11, t01, t12, t02 = [grad_t[block * atoms : (block + 1) * atoms] for block in range(5)]
     third = (t00 + t11) * (1.0 / 3.0)
     pieces = [grad_s] + [grad_v[axis * atoms : (axis + 1) * atoms] for axis in range(3)]
@@ -398,16 +408,11 @@
 
 def gather_kernel(groups, quad_ref, own_ref, _, *rest):
     message_refs, out_ref = rest[: len(groups)], rest[len(groups)]
-    atoms = own_ref.shape[0]
-    ghost = quad_ref.shape[3]
-    rows = lax.broadcasted_iota(jnp.int32, (atoms, ghost), 0)
-    total = own_ref[...]
-    for (_, cells), message_ref in zip(groups, message_refs):
-        for place, cell in enumerate(cells):
-            row, col = QUARTER[BORDER[cell][0]], QUARTER[BORDER[cell][1]]
-            chosen = (rows == quad_ref[0, row, col : col + 1, :]).astype(jnp.bfloat16)
-            total = total + dot_t(chosen, message_ref[place * ghost : (place + 1) * ghost, :], ((1,), (0,)))
-    out_ref[...] = total
+    order = [BORDER[cell] for _, cells in groups for cell in cells]
+    quarters = [(QUARTER[row], QUARTER[col]) for row, col in order]
+    chosen = quarter_onehot(quad_ref, own_ref.shape[0], quarters)
+    messages = jnp.concatenate([message_ref[...] for message_ref in message_refs], axis=0)
+    out_ref[...] = own_ref[...] + dot_t(chosen, messages, ((1,), (0,)))
 
 
 def whole(shape):
@@ -526,7 +531,7 @@
             shape_z_ref[brick, 0], shape_z_ref[brick, 1] = high, low
             return carry
 
-        lax.fori_loop(0, bricks, tables, 0, unroll=4)
+        lax.fori_loop(0, bricks, tables, 0, unroll=8)
 
     first = step * chunk
 
@@ -549,7 +554,7 @@
             lines_ref[place, line * lanes_z : (line + 1) * lanes_z] = grid[line * window : (line + 1) * window]
         return carry
 
-    lax.fori_loop(0, bricks, spread, 0, unroll=2)
+    lax.fori_loop(0, bricks, spread, 0, unroll=8)
     own = pl.multiple_of(lax.axis_index("brick") * (2 * window), 2 * window)
 
     def solve(batch, carry):

time: 70.7 us -> 67.9 us (0.960)
  Pallas kernels: 44.9 us -> 42.1 us
    pallas_call x1, Pallas kernels: 13.6 us -> 11.7 us  [potential_block(): pl.pallas_call(functools.partial(potential_kernel, cells_y), grid=(full_y...]
  transfers between devices with their start and end apart: 11 -> 11, of which waited for: 1 -> 1; matrix products, arithmetic and copies ran while one was open for 1% -> 1% of each run, Pallas kernels for 22% -> 20%
where the time goes in v3:
time: 67.9 us; the launch traced here: 67.7 us
  Pallas kernels  42.1 us (62%)
  starting transfers between devices  20 us (29%)
  local copies, waits for them, and re-layouts  3.24 us (5%)
  waiting for transfers between devices  1.33 us (2%)
  between operations  0.96 us (1%)
    pallas_call x1, Pallas kernels, per_device(): pl.pallas_call(functools.partial(layer_kernel, groups), out_shape=[jax.Sh...  24.8 us
    ppermute x10, starting transfers between devices, shifted(): return lax.ppermute(value, ('brick', 'pme'), pairs)  16.4 us
    pallas_call x1, Pallas kernels, potential_block(): pl.pallas_call(functools.partial(potential_kernel, cells_y), grid=(full_y...  11.7 us
    all_to_all x1, starting transfers between devices, all_charges(): lax.all_to_all(copies, ('brick', 'pme'), split_axis=0, concat_axis=0, til...  3.62 us
    unnamed x56, local copies, waits for them, and re-layouts  2.83 us
    pallas_call x1, Pallas kernels, per_device(): pl.pallas_call(functools.partial(gather_kernel, groups), in_specs=[pl.Blo...  1.92 us
    pallas_call x1, Pallas kernels, per_device(): pl.pallas_call(radial_kernel, out_shape=[jax.ShapeDtypeStruct((hidden_uni...  1.86 us
    pallas_call x1, Pallas kernels, per_device(): pl.pallas_call(functools.partial(pack_kernel, groups), out_shape=message_...  1.85 us
  transfers between devices with their start and end apart: 11, of which 1 were waited for; matrix products, arithmetic and copies ran while one was open for 1% of the time, Pallas kernels for 20%

profile of v3, /device:TPU:0, one launch (start us, length us, event | category | flops | bytes accessed | tf_op | source)
XLA Modules:
  0.0 67.7 jit_solution(10753869065567730533)
XLA Ops:
  0.6 0.0 copy-start.23
  0.6 1.8 %pack.1 = (bf16[32,512]{1,0:T(8,128)(2,1)}, bf16[32,512]{1,0:T(8,128)(2,1)}, bf16[64,512]{1,0:T(8,128)(2,1)}, bf16[32,512]{1,0:T(8,128)(2,1)}, bf16[32,512]{1,0:T(8,128)(2,1)}) custom-call(s32[1,2,2,16]{3,2,1,0:T(2,128)} %quad_ref.3, bf16[128,512]{1,0:T(8,128)(2,1)} %features_ref.5), custom_call_target="tpu_custom_call" | custom-call | tf_op jit(solution)/shard_map/pack/pallas_call | solution.py:647
  2.5 3.0 %collective-permute-start.2 = (bf16[64,512]{1,0:T(8,128)(2,1)}, bf16[64,512]{1,0:T(8,128)(2,1)S(1)}, u32[]{:S(2)}, u32[]{:S(2)}) collective-permute-start(bf16[64,512]{1,0:T(8,128)(2,1)} %get-tuple-element.26), channel_id=1, source_target_pairs={{1,0},{0,1},{3,2},{2,3},{5,4},{4,5},{7,6},{6,7},{9,8},{8,9},{11,10... | collective-permute-start | bytes 196616 | tf_op jit(solution)/shard_map/ppermute | solution.py:49
  5.5 0.0 collective-permute-start
  5.5 1.5 %collective-permute-start.1 = (bf16[32,512]{1,0:T(8,128)(2,1)}, bf16[32,512]{1,0:T(8,128)(2,1)S(1)}, u32[]{:S(2)}, u32[]{:S(2)}) collective-permute-start(bf16[32,512]{1,0:T(8,128)(2,1)} %get-tuple-element.25), channel_id=1, source_target_pairs={{30,0},{31,1},{0,2},{1,3},{2,4},{3,5},{4,6},{5,7},{6,8},{7,9},{8,1... | collective-permute-start | bytes 98312 | tf_op jit(solution)/shard_map/ppermute | solution.py:49
  7.0 3.8 %collective-permute-start.3 = (bf16[32,512]{1,0:T(8,128)(2,1)}, bf16[32,512]{1,0:T(8,128)(2,1)S(1)}, u32[]{:S(2)}, u32[]{:S(2)}) collective-permute-start(bf16[32,512]{1,0:T(8,128)(2,1)} %get-tuple-element.27), channel_id=1, source_target_pairs={{3,0},{2,1},{5,2},{4,3},{7,4},{6,5},{9,6},{8,7},{11,8},{10,9},{13,... | collective-permute-start | bytes 98312 | tf_op jit(solution)/shard_map/ppermute | solution.py:49
  10.8 0.7 collective-permute-start.4
  11.5 0.0 copy-done.23
  11.5 0.1 reshape.23
  11.6 0.1 copy.27
  11.6 0.0 copy-done.21
  11.6 0.0 copy-start.4
  11.7 0.0 copy-start.8
  11.7 0.0 copy-start.11
  11.7 0.0 copy-start.6
  11.7 0.0 copy-start.7
  11.7 0.2 reshape.21
  11.9 0.1 copy.26
  12.0 0.6 copy-done.4
  12.6 0.0 copy-done.8
  12.6 0.0 copy-done.11
  12.6 0.2 copy-done
  12.8 1.9 %radial.1 = (bf16[64,8192]{1,0:T(8,128)(2,1)S(1)}, f32[3,64,128]{2,1,0:T(8,128)S(1)}, bf16[896,64]{1,0:T(8,128)(2,1)S(1)}, bf16[512,128]{1,0:T(8,128)(2,1)S(1)}) custom-call(f32[3,64,128]{2,1,0:T(8,128)S(1)} %bitcast.5, s32[1,128]{1,0:T(1,128)S(1)} %bitcast.8, f32[8,64]{1,0:T(8,128)S(1)} %copy-done.8, bf16[64,896]{1,0:T(8,128)(2,1)S(1)} %copy-done.4, ...), custom_call_target="tpu_custom_call" | custom-call | tf_op jit(solution)/shard_map/radial/pallas_call | solution.py:654
  14.6 0.0 collective-permute-done.rest_0_
  14.7 0.0 collective-permute-done.1.rest_1_
  14.7 0.0 collective-permute-done.3.rest_3_
  14.7 0.0 collective-permute-done.4.rest_4_
  14.7 0.0 collective-permute-done.2.rest_2_
  14.7 0.0 copy-start.10
  14.7 0.0 copy-start.9
  14.7 0.0 copy-start.12
  14.7 0.0 copy-done.6
  14.8 0.6 copy-done.10
  15.4 0.0 copy-done.9
  15.4 0.0 copy-start.17
  15.4 0.0 copy-start.18
  15.4 0.0 copy-start.19
  15.4 24.8 %layer.1 = (bf16[128,1152]{1,0:T(8,128)(2,1)}, f32[32,8,128]{2,1,0:T(8,128)}, f32[128,512]{1,0:T(8,128)S(1)}, bf16[32,512]{1,0:T(8,128)(2,1)S(1)}, bf16[32,512]{...) custom-call(bf16[64,8192]{1,0:T(8,128)(2,1)S(1)} %get-tuple-element.20., ...), custom_call_target="tpu_custom_call" | custom-call | tf_op jit(solution)/shard_map/layer/pallas_call | solution.py:670
  40.2 0.7 %copy-done.2 = f32[128,512]{1,0:T(8,128)} copy-done((f32[128,512]{1,0:T(8,128)}, f32[128,512]{1,0:T(8,128)S(1)}, u32[]{:S(2)}) %copy-start.2) | copy-done | bytes 262168
  40.9 3.6 %all-to-all-start = ((f32[32,8,128]{2,1,0:T(8,128)}), f32[32,8,128]{2,1,0:T(8,128)S(1)}, u32[]{:S(2)}, u32[]{:S(2)}) async-start(f32[32,8,128]{2,1,0:T(8,128)} %get-tuple-element.31), calls=%async_computation | async-start | bytes 262144 | tf_op jit(solution)/shard_map/all_to_all | solution.py:615
  44.6 5.3 %collective-permute-start.5 = (bf16[32,512]{1,0:T(8,128)(2,1)S(1)}, bf16[32,512]{1,0:T(8,128)(2,1)S(1)}, u32[]{:S(2)}, u32[]{:S(2)}) collective-permute-start(bf16[32,512]{1,0:T(8,128)(2,1)S(1)} %get-tuple-element.32), channel_id=1, source_target_pairs={{3,0},{2,1},{5,2},{4,3},{7,4},{6,5},{9,6},{8,7},{11,8},{10,9},{13,... | collective-permute-start | bytes 98312 | tf_op jit(solution)/shard_map/ppermute | solution.py:49
  49.8 0.5 collective-permute-start.6
  50.4 0.1 collective-permute-start.8
  50.5 0.0 collective-permute-start.9
  50.5 1.5 %collective-permute-start.7 = (bf16[64,512]{1,0:T(8,128)(2,1)S(1)}, bf16[64,512]{1,0:T(8,128)(2,1)S(1)}, u32[]{:S(2)}, u32[]{:S(2)}) collective-permute-start(bf16[64,512]{1,0:T(8,128)(2,1)S(1)} %get-tuple-element.34), channel_id=1, source_target_pairs={{1,0},{0,1},{3,2},{2,3},{5,4},{4,5},{7,6},{6,7},{9,8},{8,9},{11,10... | collective-permute-start | bytes 196616 | tf_op jit(solution)/shard_map/ppermute | solution.py:49
  52.0 1.3 %all-to-all-done = f32[32,8,128]{2,1,0:T(8,128)S(1)} async-done(((f32[32,8,128]{2,1,0:T(8,128)}), f32[32,8,128]{2,1,0:T(8,128)S(1)}, u32[]{:S(2)}, u32[]{:S(2)}) %all-to-all-start) | async-done | bytes 131104 | tf_op jit(solution)/shard_map/all_to_all | solution.py:615
  53.3 0.0 copy-done.17
  53.3 0.0 copy-done.18
  53.3 0.0 copy-done.19
  53.3 0.0 copy-done.13
  53.3 0.0 copy-done.20
  53.3 11.7 %potential.1._ = f32[6,24,192]{2,1,0:T(8,128)} custom-call(f32[16,2,8,128]{3,2,1,0:T(8,128)S(1)} %bitcast.7, bf16[512,192]{1,0:T(8,128)(2,1)S(1)} %copy-done.14, bf16[96,48]{1,0:T(8,128)(2,1)S(1)} %copy-done.19, bf16[192,128]{1,0:T(8,128)(2,1)S(1)} %copy-done.17, bf16[256,96]{1,0:T(8,128)(2,1)S(1)} %copy-done.15, f32[48,48]{1,0:T(8,128)S(1)} %copy-done.18, ...), custom_call_target="tpu_custom_call" | custom-call | flops 20000000000 | bytes 10000000 | tf_op jit(solution)/shard_map/potential/pallas_call | solution.py:595
  65.1 0.0 collective-permute-done.5.rest_0_
  65.1 0.0 collective-permute-done.6.rest_1_
  65.1 0.0 collective-permute-done.8.rest_3_
  65.1 0.0 copy-start.26
  65.1 0.0 collective-permute-done.9.rest_4_
  65.1 0.0 collective-permute-done.7.rest_2_
  65.1 0.5 copy-done.24
  65.7 0.0 copy-done.25
  65.7 0.0 copy-done.26
  65.7 0.0 copy-done.27
  65.7 0.0 copy-done.22
  65.8 1.9 %gather.1 = f32[128,512]{1,0:T(8,128)} custom-call(s32[1,2,2,16]{3,2,1,0:T(2,128)} %quad_ref.3, f32[128,512]{1,0:T(8,128)} %copy-done.2, f32[6,24,192]{2,1,0:T(8,128)} %potential.1._, bf16[32,512]{1,0:T(8,128)(2,1)} %copy-done.24, bf16[32,512]{1,0:T(8,128)(2,1)} %copy-done.25, bf16[64,512]{1,0:T(8,128)(2,1)} %copy-done.22, bf16[32,512]{1,0:T(8,128)(2,1)} %copy-done.26, ...), custom_call_target="tpu_custom_call" | custom-call | tf_op jit(solution)/shard_map/gather/pallas_call | solution.py:714
  (23 shorter events, 0.0 us)
Async XLA Ops:
  0.6 10.9 %copy-start.23 = (s32[8192]{0:T(1024)S(1)}, s32[8192]{0:T(1024)}, u32[]{:S(2)}) copy-start(s32[8192]{0:T(1024)} %param.25) | copy-start | bytes 98308
  2.5 9.2 %copy-start.21 = (f32[3,8192]{1,0:T(4,128)S(1)}, f32[3,8192]{1,0:T(4,128)}, u32[]{:S(2)}) copy-start(f32[3,8192]{1,0:T(4,128)} %param.27) | copy-start | bytes 294916
  2.5 12.2 %collective-permute-start.2 = (bf16[64,512]{1,0:T(8,128)(2,1)}, bf16[64,512]{1,0:T(8,128)(2,1)S(1)}, u32[]{:S(2)}, u32[]{:S(2)}) collective-permute-start(bf16[64,512]{1,0:T(8,128)(2,1)} %get-tuple-element.26), channel_id=1, source_target_pairs={{1,0},{0,1},{3,2},{2,3},{5,4},{4,5},{7,6},{6,7},{9,8},{8,9},{11,10... | collective-permute-start | bytes 196616 | tf_op jit(solution)/shard_map/ppermute | solution.py:49
  5.5 9.2 %collective-permute-start = (bf16[32,512]{1,0:T(8,128)(2,1)}, bf16[32,512]{1,0:T(8,128)(2,1)S(1)}, u32[]{:S(2)}, u32[]{:S(2)}) collective-permute-start(bf16[32,512]{1,0:T(8,128)(2,1)} %get-tuple-element.24), channel_id=1, source_target_pairs={{31,0},{30,1},{1,2},{0,3},{3,4},{2,5},{5,6},{4,7},{7,8},{6,9},{9,1... | collective-permute-start | bytes 98312 | tf_op jit(solution)/shard_map/ppermute | solution.py:49
  5.5 9.2 %collective-permute-start.1 = (bf16[32,512]{1,0:T(8,128)(2,1)}, bf16[32,512]{1,0:T(8,128)(2,1)S(1)}, u32[]{:S(2)}, u32[]{:S(2)}) collective-permute-start(bf16[32,512]{1,0:T(8,128)(2,1)} %get-tuple-element.25), channel_id=1, source_target_pairs={{30,0},{31,1},{0,2},{1,3},{2,4},{3,5},{4,6},{5,7},{6,8},{7,9},{8,1... | collective-permute-start | bytes 98312 | tf_op jit(solution)/shard_map/ppermute | solution.py:49
  7.0 7.7 %collective-permute-start.3 = (bf16[32,512]{1,0:T(8,128)(2,1)}, bf16[32,512]{1,0:T(8,128)(2,1)S(1)}, u32[]{:S(2)}, u32[]{:S(2)}) collective-permute-start(bf16[32,512]{1,0:T(8,128)(2,1)} %get-tuple-element.27), channel_id=1, source_target_pairs={{3,0},{2,1},{5,2},{4,3},{7,4},{6,5},{9,6},{8,7},{11,8},{10,9},{13,... | collective-permute-start | bytes 98312 | tf_op jit(solution)/shard_map/ppermute | solution.py:49
  10.8 3.9 %collective-permute-start.4 = (bf16[32,512]{1,0:T(8,128)(2,1)}, bf16[32,512]{1,0:T(8,128)(2,1)S(1)}, u32[]{:S(2)}, u32[]{:S(2)}) collective-permute-start(bf16[32,512]{1,0:T(8,128)(2,1)} %get-tuple-element.28), channel_id=1, source_target_pairs={{2,0},{3,1},{4,2},{5,3},{6,4},{7,5},{8,6},{9,7},{10,8},{11,9},{12,... | collective-permute-start | bytes 98312 | tf_op jit(solution)/shard_map/ppermute | solution.py:49
  11.6 0.9 %copy-start.4 = (bf16[64,896]{1,0:T(8,128)(2,1)S(1)}, bf16[64,896]{1,0:T(8,128)(2,1)}, u32[]{:S(2)}) copy-start(bf16[64,896]{1,0:T(8,128)(2,1)} %weight_radial_ref.1) | copy-start | bytes 344068
  11.7 0.9 %copy-start.8 = (f32[8,64]{1,0:T(8,128)S(1)}, f32[8,64]{1,0:T(8,128)}, u32[]{:S(2)}) copy-start(f32[8,64]{1,0:T(8,128)} %basis_weight_ref.1) | copy-start | bytes 6148
  11.7 0.9 %copy-start.11 = (s32[128]{0:T(128)S(1)}, s32[128]{0:T(128)}, u32[]{:S(2)}) copy-start(s32[128]{0:T(128)} %param.26) | copy-start | bytes 1540
  11.7 3.1 %copy-start.6 = (f32[128,128]{1,0:T(8,128)S(1)}, f32[128,128]{1,0:T(8,128)}, u32[]{:S(2)}) copy-start(f32[128,128]{1,0:T(8,128)} %weight_vector_ref.1) | copy-start | bytes 196612
  11.7 3.1 %copy-start.7 = (f32[128,128]{1,0:T(8,128)S(1)}, f32[128,128]{1,0:T(8,128)}, u32[]{:S(2)}) copy-start(f32[128,128]{1,0:T(8,128)} %weight_tensor_ref.1) | copy-start | bytes 196612
  11.9 0.9 %copy-start = (bf16[128,512]{1,0:T(8,128)(2,1)S(1)}, bf16[128,512]{1,0:T(8,128)(2,1)}, u32[]{:S(2)}) copy-start(bf16[128,512]{1,0:T(8,128)(2,1)} %features_ref.5) | copy-start | bytes 393220
  11.9 2.9 %copy-start.1 = (bf16[128,1152]{1,0:T(8,128)(2,1)S(1)}, bf16[128,1152]{1,0:T(8,128)(2,1)}, u32[]{:S(2)}) copy-start(bf16[128,1152]{1,0:T(8,128)(2,1)} %cotangent_ref.1) | copy-start | bytes 884740
  12.8 2.0 %copy-start.3 = (f32[128,256]{1,0:T(8,128)S(1)}, f32[128,256]{1,0:T(8,128)}, u32[]{:S(2)}) copy-start(f32[128,256]{1,0:T(8,128)} %weight_gate_ref.1) | copy-start | bytes 393220
  12.8 2.0 %copy-start.5 = (f32[128,128]{1,0:T(8,128)S(1)}, f32[128,128]{1,0:T(8,128)}, u32[]{:S(2)}) copy-start(f32[128,128]{1,0:T(8,128)} %weight_scalar_ref.1) | copy-start | bytes 196612
  14.7 0.7 %copy-start.10 = (f32[3,128]{1,0:T(4,128)S(1)}, f32[3,128]{1,0:T(4,128)}, u32[]{:S(2)}) copy-start(f32[3,128]{1,0:T(4,128)} %grid_frac_ref.1) | copy-start | bytes 4612
  14.7 0.7 %copy-start.9 = (s32[3,128]{1,0:T(4,128)S(1)}, s32[3,128]{1,0:T(4,128)}, u32[]{:S(2)}) copy-start(s32[3,128]{1,0:T(4,128)} %grid_base_ref.1) | copy-start | bytes 4612
  14.7 0.7 %copy-start.12 = (f32[128]{0:T(128)S(1)}, f32[128]{0:T(128)}, u32[]{:S(2)}) copy-start(f32[128]{0:T(128)} %param.35) | copy-start | bytes 1540
  15.4 37.9 %copy-start.14 = (bf16[512,192]{1,0:T(8,128)(2,1)S(1)}, bf16[512,192]{1,0:T(8,128)(2,1)}, u32[]{:S(2)}) copy-start(bf16[512,192]{1,0:T(8,128)(2,1)} %constant.16.clone.wave_z_ref) | copy-start | bytes 589828
  15.4 37.9 %copy-start.15 = (bf16[256,96]{1,0:T(8,128)(2,1)S(1)}, bf16[256,96]{1,0:T(8,128)(2,1)}, u32[]{:S(2)}) copy-start(bf16[256,96]{1,0:T(8,128)(2,1)} %constant.19.clone.own_x_ref) | copy-start | bytes 147460
  15.4 37.9 %copy-start.16 = (f32[96,1]{1,0:T(8,128)S(1)}, f32[96,1]{1,0:T(8,128)}, u32[]{:S(2)}) copy-start(f32[96,1]{1,0:T(8,128)} %constant.22.clone.square_x_ref) | copy-start | bytes 1156
  15.4 37.9 %copy-start.17 = (bf16[192,128]{1,0:T(8,128)(2,1)S(1)}, bf16[192,128]{1,0:T(8,128)(2,1)}, u32[]{:S(2)}) copy-start(bf16[192,128]{1,0:T(8,128)(2,1)} %constant.18.clone.wave_x_ref) | copy-start | bytes 147460
  15.4 37.9 %copy-start.18 = (f32[48,48]{1,0:T(8,128)S(1)}, f32[48,48]{1,0:T(8,128)}, u32[]{:S(2)}) copy-start(f32[48,48]{1,0:T(8,128)} %constant.20.clone.own_y_ref) | copy-start | bytes 27652
  15.4 37.9 %copy-start.19 = (bf16[96,48]{1,0:T(8,128)(2,1)S(1)}, bf16[96,48]{1,0:T(8,128)(2,1)}, u32[]{:S(2)}) copy-start(bf16[96,48]{1,0:T(8,128)(2,1)} %constant.17.clone.wave_y_ref) | copy-start | bytes 27652
  40.2 0.7 %copy-start.2 = (f32[128,512]{1,0:T(8,128)}, f32[128,512]{1,0:T(8,128)S(1)}, u32[]{:S(2)}) copy-start(f32[128,512]{1,0:T(8,128)S(1)} %get-tuple-element.30.own_ref) | copy-start | bytes 786436
  40.9 12.4 %copy-start.13 = (f32[256,192]{1,0:T(8,128)S(1)}, f32[256,192]{1,0:T(8,128)}, u32[]{:S(2)}) copy-start(f32[256,192]{1,0:T(8,128)} %constant.21.clone.own_z_ref) | copy-start | bytes 589828
  40.9 12.4 %all-to-all-start = ((f32[32,8,128]{2,1,0:T(8,128)}), f32[32,8,128]{2,1,0:T(8,128)S(1)}, u32[]{:S(2)}, u32[]{:S(2)}) async-start(f32[32,8,128]{2,1,0:T(8,128)} %get-tuple-element.31), calls=%async_computation | async-start | bytes 262144 | tf_op jit(solution)/shard_map/all_to_all | solution.py:615
  44.6 20.5 %collective-permute-start.5 = (bf16[32,512]{1,0:T(8,128)(2,1)S(1)}, bf16[32,512]{1,0:T(8,128)(2,1)S(1)}, u32[]{:S(2)}, u32[]{:S(2)}) collective-permute-start(bf16[32,512]{1,0:T(8,128)(2,1)S(1)} %get-tuple-element.32), channel_id=1, source_target_pairs={{3,0},{2,1},{5,2},{4,3},{7,4},{6,5},{9,6},{8,7},{11,8},{10,9},{13,... | collective-permute-start | bytes 98312 | tf_op jit(solution)/shard_map/ppermute | solution.py:49
  49.8 15.2 %collective-permute-start.6 = (bf16[32,512]{1,0:T(8,128)(2,1)S(1)}, bf16[32,512]{1,0:T(8,128)(2,1)S(1)}, u32[]{:S(2)}, u32[]{:S(2)}) collective-permute-start(bf16[32,512]{1,0:T(8,128)(2,1)S(1)} %get-tuple-element.33), channel_id=1, source_target_pairs={{2,0},{3,1},{4,2},{5,3},{6,4},{7,5},{8,6},{9,7},{10,8},{11,9},{12,... | collective-permute-start | bytes 98312 | tf_op jit(solution)/shard_map/ppermute | solution.py:49
  50.4 14.7 %collective-permute-start.8 = (bf16[32,512]{1,0:T(8,128)(2,1)S(1)}, bf16[32,512]{1,0:T(8,128)(2,1)S(1)}, u32[]{:S(2)}, u32[]{:S(2)}) collective-permute-start(bf16[32,512]{1,0:T(8,128)(2,1)S(1)} %get-tuple-element.35), channel_id=1, source_target_pairs={{31,0},{30,1},{1,2},{0,3},{3,4},{2,5},{5,6},{4,7},{7,8},{6,9},{9,1... | collective-permute-start | bytes 98312 | tf_op jit(solution)/shard_map/ppermute | solution.py:49
  50.5 14.6 %collective-permute-start.9 = (bf16[32,512]{1,0:T(8,128)(2,1)S(1)}, bf16[32,512]{1,0:T(8,128)(2,1)S(1)}, u32[]{:S(2)}, u32[]{:S(2)}) collective-permute-start(bf16[32,512]{1,0:T(8,128)(2,1)S(1)} %get-tuple-element.36), channel_id=1, source_target_pairs={{30,0},{31,1},{0,2},{1,3},{2,4},{3,5},{4,6},{5,7},{6,8},{7,9},{8,1... | collective-permute-start | bytes 98312 | tf_op jit(solution)/shard_map/ppermute | solution.py:49
  50.5 2.9 %copy-start.20 = (f32[1,256]{1,0:T(1,128)S(1)}, f32[1,256]{1,0:T(1,128)}, u32[]{:S(2)}) copy-start(f32[1,256]{1,0:T(1,128)} %constant.23.clone.square_z_ref) | copy-start | bytes 3076
  50.5 14.6 %collective-permute-start.7 = (bf16[64,512]{1,0:T(8,128)(2,1)S(1)}, bf16[64,512]{1,0:T(8,128)(2,1)S(1)}, u32[]{:S(2)}, u32[]{:S(2)}) collective-permute-start(bf16[64,512]{1,0:T(8,128)(2,1)S(1)} %get-tuple-element.34), channel_id=1, source_target_pairs={{1,0},{0,1},{3,2},{2,3},{5,4},{4,5},{7,6},{6,7},{9,8},{8,9},{11,10... | collective-permute-start | bytes 196616 | tf_op jit(solution)/shard_map/ppermute | solution.py:49
  65.1 0.6 copy-start.24
  65.1 0.6 copy-start.25
  65.1 0.6 copy-start.26
  65.1 0.6 copy-start.27
  65.1 0.6 copy-start.22
